TPU v7x, 256 devices: a whole 4x4x8 slice. The times are simulated.
256 devices in a mesh: row: 64 (over x, z, core), col: 4 (over y).
Axes of the slice: x: 4, y: 4, z: 8, core: 2. Of those that a mesh axis runs over, the one named last changes fastest.
Arguments:
- query_grads: bfloat16 [4, 8192, 28672], P(None, 'row', 'col'), may hold values from -0.00036621094 to 0.00036621094
- out_grads: bfloat16 [1024, 8192], P('col', 'row'), may hold values from -6 to 6
- activations: bfloat16 [1024, 28672], P('row', 'col'), may hold values from -6 to 6
- seq_ids: int32 [1024], P('row'), may hold values from 0 to 31, never falling along the last dimension, each value on 1 to 64 neighbouring positions
Outputs:
- scores: float32 [1024, 4], P('row')
- seq_scores: float32 [32, 4], replicated
Inputs may be any that keep to these rules, and one draw needn't show every extreme that they name: `seq_ids`: non-decreasing along the tokens; every sequence holds between 1 and 64 tokens.
All inputs are finite; a program needn't handle non-finite values.
Results may differ from a plain program's by a relative error of at most 0.0003.
Values may be sent and summed in bfloat16 or wider, within the bound.
No kernel may reach another device: no remote copies, remote signals or barrier semaphores. Data moves between devices by JAX's collectives and lax.ppermute only.
A program may use at most 64 MiB of HBM per device.

v0:
```python
import functools

import jax
import jax.numpy as jnp
import numpy as np
from jax import lax
from jax.experimental import pallas as pl
from jax.experimental.pallas import tpu as pltpu
from jax.sharding import PartitionSpec as P

EXACT = lax.Precision.HIGHEST
WORK = 256
NX, NZ = 4, 8


def cat(parts, axis=0):
    return parts[0] if len(parts) == 1 else jnp.concatenate(parts, axis)


def shift(block, dx, dz):
    pairs = [
        ((x * NZ + z) * 2 + c, ((x + dx) % NX * NZ + (z + dz) % NZ) * 2 + c)
        for x in range(NX)
        for z in range(NZ)
        for c in range(2)
    ]
    return lax.ppermute(block, "row", pairs)


def swap(block):
    return lax.ppermute(block, "row", [(i, i ^ 1) for i in range(NX * NZ * 2)])


def from_col(block, ahead, cols):
    return lax.ppermute(block, "col", [(i, (i - ahead) % cols) for i in range(cols)])


L, H, F = (0,), (1,), (0, 1)
E = (1, 0), (-1, 0), (0, 1), (0, -1)
ROUNDS = [
    [(d, [((0, 0), F, d)]) for d in E],
    [
        (E[0], [((1, 0), L, (2, 0)), ((0, 1), F, (1, 1))]),
        (E[1], [((-1, 0), H, (2, 0)), ((0, -1), F, (-1, -1))]),
        (E[2], [((0, 1), F, (0, 2)), ((-1, 0), F, (-1, 1))]),
        (E[3], [((0, -1), F, (0, -2)), ((1, 0), F, (1, -1))]),
    ],
    [
        (E[0], [((1, 1), L, (2, 1)), ((1, -1), L, (2, -1)), ((0, 2), F, (1, 2))]),
        (E[1], [((-1, 1), H, (2, 1)), ((-1, -1), H, (2, -1)), ((0, -2), F, (-1, -2))]),
        (E[2], [((0, 2), F, (0, 3)), ((-1, 1), F, (-1, 2))]),
        (E[3], [((0, -2), F, (0, -3)), ((1, -1), F, (1, -2))]),
    ],
    [
        (E[0], [((1, 2), L, (2, 2)), ((1, -2), L, (2, -2)), ((0, 3), F, (1, 3))]),
        (E[1], [((-1, 2), H, (2, 2)), ((-1, -2), H, (2, -2)), ((0, -3), F, (-1, -3))]),
        (E[2], [((0, 3), L, (0, 4)), ((-1, 2), F, (-1, 3))]),
        (E[3], [((0, -3), H, (0, 4)), ((1, -2), F, (1, -3))]),
    ],
    [
        (E[0], [((1, 3), L, (2, 3)), ((1, -3), L, (2, -3))]),
        (E[1], [((-1, 3), H, (2, 3)), ((-1, -3), H, (2, -3))]),
        (E[2], [((1, 3), L, (1, 4)), ((-1, 3), L, (-1, 4))]),
        (E[3], [((1, -3), H, (1, 4)), ((-1, -3), H, (-1, 4))]),
        ((1, 1), [((1, 3), F, (2, 4))]),
    ],
]


def scores_kernel(places, sizes, where, q_mine, q_other, *refs):
    slices, pieces = refs[:2], refs[2 : 2 + len(sizes)]
    out, seq, a_buf, g_buf, w_buf, a_sem, g_sem = refs[2 + len(sizes) :]
    queries, rows, half = q_other.shape
    tokens = sum(sizes) // len(places)
    g_copies = [
        pltpu.make_async_copy(g, g_buf.at[k], g_sem.at[k]) for k, g in enumerate(slices)
    ]
    count, a_copies = 0, []
    for i, (piece, size) in enumerate(zip(pieces, sizes)):
        a_copies.append(
            pltpu.make_async_copy(piece, a_buf.at[pl.ds(count, size)], a_sem.at[i])
        )
        count += size
    for copy in g_copies + a_copies:
        copy.start()
    for copy in g_copies:
        copy.wait()
    for i, ((ox, oz), h) in enumerate(places):
        u = lax.rem(where[0] + (NX - ox), NX)
        v = lax.rem(where[1] + (NZ - oz), NZ)
        at = pl.multiple_of(((u % 2 * NZ + v) * 2 + h) * tokens, tokens)
        w_buf[pl.ds(i * tokens, tokens)] = g_buf[u // 2, pl.ds(at, tokens)]
    weights = w_buf[...].astype(jnp.float32).T
    for copy in a_copies:
        copy.wait()
    total = [jnp.zeros((1, count), jnp.float32) for _ in range(queries)]
    for p, grads in enumerate((q_mine, q_other)):
        inner = lax.dot_general(
            grads[...].reshape(queries * rows, half),
            a_buf[:, :half],
            (((1,), (1,)), ((), ())),
            preferred_element_type=jnp.float32,
        )
        for q in range(queries):
            weighed = inner[q * rows : (q + 1) * rows] * weights[p * rows : (p + 1) * rows]
            total[q] = total[q] + jnp.sum(weighed, axis=0, keepdims=True)
    scores = jnp.concatenate(total + [jnp.zeros((8 - queries, count), jnp.float32)], 0)
    out[...] = scores
    ids = a_buf[:, half:].astype(jnp.float32)
    lane = lax.broadcasted_iota(jnp.int32, (count, 128), 1).astype(jnp.float32)
    onehot = jnp.where(ids == lane, 1.0, 0.0)
    seq[...] = jnp.dot(scores, onehot, precision=EXACT, preferred_element_type=jnp.float32)


def piece_scores(where, q_mine, q_other, slices, pieces, places):
    sizes = [piece.shape[0] for piece in pieces]
    count = sum(sizes)
    queries, rows, half = q_other.shape
    anywhere = pl.BlockSpec(memory_space=pl.ANY)
    whole = pl.BlockSpec(memory_space=pltpu.VMEM)
    return pl.pallas_call(
        functools.partial(scores_kernel, places, sizes),
        out_shape=(
            jax.ShapeDtypeStruct((8, count), jnp.float32),
            jax.ShapeDtypeStruct((8, 128), jnp.float32),
        ),
        in_specs=[pl.BlockSpec(memory_space=pltpu.SMEM)]
        + [whole] * 2
        + [anywhere] * (2 + len(pieces)),
        out_specs=[whole, whole],
        scratch_shapes=[
            pltpu.VMEM((count, half + 128), jnp.bfloat16),
            pltpu.VMEM((2,) + slices[0].shape, jnp.bfloat16),
            pltpu.VMEM((count, 2 * rows), jnp.bfloat16),
            pltpu.SemaphoreType.DMA((len(pieces),)),
            pltpu.SemaphoreType.DMA((2,)),
        ],
        compiler_params=pltpu.CompilerParams(vmem_limit_bytes=16 << 20),
        cost_estimate=pl.CostEstimate(
            flops=4 * queries * rows * half * count,
            bytes_accessed=4 * queries * rows * half + 2 * half * count,
            transcendentals=0,
        ),
        name="scores",
    )(where, q_mine, q_other, *slices, *pieces)


def body(query_grads, out_grads, activations, seq_ids):
    queries, rows_here, width = query_grads.shape
    half = width // 2
    tokens = seq_ids.shape[0]
    rows, cols = lax.axis_size("row"), lax.axis_size("col")
    seq_count = max(tokens * rows // 32, 4)
    row, y = lax.axis_index("row"), lax.axis_index("col")
    core, z, x = lax.rem(row, 2), lax.rem(lax.div(row, 2), NZ), lax.div(row, 2 * NZ)
    where = jnp.stack([lax.rem(x + cols - y, NX), z])

    def columns(array, which):
        start = (0,) * (array.ndim - 1) + (which * half,)
        return lax.dynamic_slice(array, start, array.shape[:-1] + (half,))

    ids = jnp.broadcast_to(seq_ids[:, None].astype(activations.dtype), (tokens, 128))
    mine = cat([columns(activations, core), ids], 1)
    other = swap(cat([columns(activations, 1 - core), ids], 1))
    own = jnp.where(core == 0, cat([mine, other]), cat([other, mine]))

    own, where, query_grads = lax.optimization_barrier((own, where, query_grads))

    q_other = columns(query_grads, 1 - core)
    slices = cat([out_grads, swap(out_grads)], 1)
    slices, _ = lax.optimization_barrier((slices, own))
    slices = cat([slices, from_col(slices, 1, cols)])

    held = {((0, 0), h): own[h * tokens : (h + 1) * tokens] for h in F}
    slots, scores, by_seq = [], [], []
    waiting = [(own, [((0, 0), h) for h in F])]

    def work():
        count, pieces, places = 0, [], []
        while waiting and count + waiting[0][0].shape[0] <= WORK:
            piece, names = waiting.pop(0)
            pieces.append(piece)
            places.extend(names)
            count += piece.shape[0]
        part, seq = piece_scores(where, q_mine, q_other, slices, pieces, places)
        scores.append(part)
        by_seq.append(seq)
        slots.extend(places)

    for number, moves in enumerate(ROUNDS):
        sent = [cat([cat([held[src, h] for h in part]) for src, part, _ in load]) for _, load in moves]
        if number == 1:
            sent, slices, q_other, query_grads = lax.optimization_barrier(
                (sent, slices, q_other, query_grads)
            )
            q_other, q_mine = swap(q_other), columns(query_grads, core)
        if number == 2:
            sent, slices, q_other, q_mine = lax.optimization_barrier(
                (sent, slices, q_other, q_mine)
            )
            slices = [slices, from_col(slices, 2, cols)]
        if number > 2:
            sent, scores[-1] = lax.optimization_barrier((sent, scores[-1]))
        if number > 1:
            work()
        for ((dx, dz), load), block in zip(moves, sent):
            came = shift(block, dx, dz)
            names = [(dst, h) for _, part, dst in load for h in part]
            for i, name in enumerate(names):
                held[name] = came[i * tokens : (i + 1) * tokens]
            waiting.append((came, names))
    while waiting:
        work()

    partial = cat(scores, 1)[:queries]
    partial_seq = sum(by_seq[1:], by_seq[0])[:queries, :seq_count]
    far = np.array([(NX - ox, NZ - oz, h) for (ox, oz), h in slots], np.int32).T
    owner = (lax.rem(x + far[0], NX) * NZ + lax.rem(z + far[1], NZ)) * 2 + far[2]
    place = owner[:, None] == jnp.arange(rows, dtype=jnp.int32)[None, :]
    mine = jnp.einsum(
        "qst,so->oqt",
        partial.reshape(queries, rows, tokens),
        place.astype(jnp.float32),
        precision=EXACT,
    ).reshape(rows, -1)
    parts = cat(
        [mine, jnp.broadcast_to(partial_seq.reshape(1, -1), (rows, queries * seq_count))], 1
    )
    parts = jnp.broadcast_to(parts[:, None, :], (rows, cols, parts.shape[1]))
    parts = parts.reshape(rows * cols, -1)
    arrived = lax.all_to_all(parts, ("row", "col"), 0, 0, tiled=True)
    total = jnp.sum(arrived, axis=0)
    split = queries * tokens
    scores = total[:split].reshape(queries, tokens).T
    seq_scores = total[split:].reshape(queries, seq_count).T
    return (scores, seq_scores)


def solution(mesh):
    placed = (P(None, "row", "col"), P("col", "row"), P("row", "col"), P("row"))
    return jax.shard_map(
        body, mesh=mesh, in_specs=placed, out_specs=(P("row", None), P()), check_vma=False
    )
```

profile of v0, /device:TPU:1, one launch (start us, length us, event | category | flops | bytes accessed | tf_op | source)
XLA Modules:
  0.0 118.9 jit_solution(5928703926215897738)
XLA Ops:
  0.6 0.7 convert_element_type.5
  1.3 1.0 constant_dynamic-slice_fusion.3
  2.4 3.3 %collective-permute-start = (bf16[16,3712]{1,0:T(8,128)(2,1)S(1)}, bf16[16,3712]{1,0:T(8,128)(2,1)S(1)}, u32[]{:S(2)}, u32[]{:S(2)}) collective-permute-start(bf16[16,3712]{1,0:T(8,128)(2,1)S(1)} %pad_maximum_fusion.15), channel_id=1, source_target_pairs={{0,4},{4,0},{8,12},{12,8},{16,20},{20,16},{24,28},{28,24},{32,36},... | collective-permute-start | bytes 356360 | tf_op jit(solution)/shard_map/ppermute | solution.py:31
  5.7 0.1 collective-permute-start.5
  5.8 0.1 pad_add_fusion.where
  5.9 1.3 %collective-permute-done.5 = bf16[256,128]{1,0:T(8,128)(2,1)S(1)} collective-permute-done((bf16[256,128]{1,0:T(8,128)(2,1)}, bf16[256,128]{1,0:T(8,128)(2,1)S(1)}, u32[]{:S(2)}, u32[]{:S(2)}) %collective-permute-start.5) | collective-permute-done | bytes 65568 | tf_op jit(solution)/shard_map/ppermute | solution.py:31
  7.2 0.9 pad_maximum_fusion.14
  8.1 0.1 collective-permute-start.2
  8.2 2.4 %collective-permute-start.3 = (bf16[32,3712]{1,0:T(8,128)(2,1)S(1)}, bf16[32,3712]{1,0:T(8,128)(2,1)S(1)}, u32[]{:S(2)}, u32[]{:S(2)}) collective-permute-start(bf16[32,3712]{1,0:T(8,128)(2,1)S(1)} %maximum_select_fusion.refs_2_), channel_id=1, source_target_pairs={{0,192},{4,196},{8,200},{12,204},{16,208},{20,212},{24,216},{28,22... | collective-permute-start | bytes 712712 | tf_op jit(solution)/shard_map/ppermute | solution.py:27
  10.5 4.0 %collective-permute-start.4 = (bf16[32,3712]{1,0:T(8,128)(2,1)S(1)}, bf16[32,3712]{1,0:T(8,128)(2,1)S(1)}, u32[]{:S(2)}, u32[]{:S(2)}) collective-permute-start(bf16[32,3712]{1,0:T(8,128)(2,1)S(1)} %maximum_select_fusion.refs_2_), channel_id=1, source_target_pairs={{0,56},{4,60},{8,0},{12,4},{16,8},{20,12},{24,16},{28,20},{32,24},... | collective-permute-start | bytes 712712 | tf_op jit(solution)/shard_map/ppermute | solution.py:27
  14.6 2.7 %collective-permute-start.6 = (bf16[256,256]{1,0:T(8,128)(2,1)S(1)}, bf16[256,256]{1,0:T(8,128)(2,1)S(1)}, u32[]{:S(2)}, u32[]{:S(2)}) collective-permute-start(bf16[256,256]{1,0:T(8,128)(2,1)S(1)} %pad_maximum_fusion.14), channel_id=1, source_target_pairs={{0,3},{1,0},{2,1},{3,2},{4,7},{5,4},{6,5},{7,6},{8,11},{9,8},{10,9... | collective-permute-start | bytes 393224 | tf_op jit(solution)/shard_map/ppermute | solution.py:35
  17.3 2.4 %constant_dynamic-slice_fusion.1 = bf16[4,128,3584]{2,1,0:T(8,128)(2,1)S(1)} fusion(bf16[4,128,7168]{2,1,0:T(8,128)(2,1)} %param.7, s32[]{:T(128)S(6)} %select_n.18), kind=kLoop, calls=%fused_computation.31 | loop fusion | bytes 7340036 | tf_op jit(solution)/shard_map/dynamic_slice | solution.py:160
  20.0 1.4 %collective-permute-start.11 = (bf16[4,128,3584]{2,1,0:T(8,128)(2,1)S(1)}, bf16[4,128,3584]{2,1,0:T(8,128)(2,1)S(1)}, u32[]{:S(2)}, u32[]{:S(2)}) collective-permute-start(bf16[4,128,3584]{2,1,0:T(8,128)(2,1)S(1)} %constant_dynamic-slice_fusion.1), channel_id=1, source_target_pairs={{0,4},{4,0},{8,12},{12,8},{16,20},{20,16},{24,28},{28,24},{32,36},... | collective-permute-start | bytes 11010056 | tf_op jit(solution)/shard_map/ppermute | solution.py:31
  21.4 2.9 %collective-permute-start.8 = (bf16[64,3712]{1,0:T(8,128)(2,1)S(1)}, bf16[64,3712]{1,0:T(8,128)(2,1)S(1)}, u32[]{:S(2)}, u32[]{:S(2)}) collective-permute-start(bf16[64,3712]{1,0:T(8,128)(2,1)S(1)} %pad_maximum_fusion.1), channel_id=1, source_target_pairs={{0,56},{4,60},{8,0},{12,4},{16,8},{20,12},{24,16},{28,20},{32,24},... | collective-permute-start | bytes 1425416 | tf_op jit(solution)/shard_map/ppermute | solution.py:27
  24.3 2.6 %collective-permute-start.10 = (bf16[48,3712]{1,0:T(8,128)(2,1)S(1)}, bf16[48,3712]{1,0:T(8,128)(2,1)S(1)}, u32[]{:S(2)}, u32[]{:S(2)}) collective-permute-start(bf16[48,3712]{1,0:T(8,128)(2,1)S(1)} %pad_maximum_fusion.7), channel_id=1, source_target_pairs={{0,192},{4,196},{8,200},{12,204},{16,208},{20,212},{24,216},{28,22... | collective-permute-start | bytes 1069064 | tf_op jit(solution)/shard_map/ppermute | solution.py:27
  26.9 0.2 constant_dynamic-slice_fusion.q_mine
  27.1 7.1 %collective-permute-done.10.refs_8_ = bf16[48,3712]{1,0:T(8,128)(2,1)S(1)} collective-permute-done((bf16[48,3712]{1,0:T(8,128)(2,1)S(1)}, bf16[48,3712]{1,0:T(8,128)(2,1)S(1)}, u32[]{:S(2)}, u32[]{:S(2)}) %collective-permute-start.10) | collective-permute-done | bytes 356384 | tf_op jit(solution)/shard_map/ppermute | solution.py:27
  34.2 3.1 %collective-permute-done.7.refs_7_ = bf16[48,3712]{1,0:T(8,128)(2,1)S(1)} collective-permute-done((bf16[48,3712]{1,0:T(8,128)(2,1)S(1)}, bf16[48,3712]{1,0:T(8,128)(2,1)S(1)}, u32[]{:S(2)}, u32[]{:S(2)}) %collective-permute-start.7) | collective-permute-done | bytes 356384 | tf_op jit(solution)/shard_map/ppermute | solution.py:27
  37.3 0.2 collective-permute-done.9.refs_2_
  37.8 0.1 collective-permute-start.14
  37.9 3.0 %collective-permute-start.16 = (bf16[512,256]{1,0:T(8,128)(2,1)S(1)}, bf16[512,256]{1,0:T(8,128)(2,1)S(1)}, u32[]{:S(2)}, u32[]{:S(2)}) collective-permute-start(bf16[512,256]{1,0:T(8,128)(2,1)S(1)} %pad_maximum_fusion.13.refs_0_), channel_id=1, source_target_pairs={{0,2},{1,3},{2,0},{3,1},{4,6},{5,7},{6,4},{7,5},{8,10},{9,11},{10,... | collective-permute-start | bytes 786440 | tf_op jit(solution)/shard_map/ppermute | solution.py:35
  40.9 2.6 %collective-permute-start.13 = (bf16[64,3712]{1,0:T(8,128)(2,1)S(1)}, bf16[64,3712]{1,0:T(8,128)(2,1)S(1)}, u32[]{:S(2)}, u32[]{:S(2)}) collective-permute-start(bf16[64,3712]{1,0:T(8,128)(2,1)S(1)} %collective-permute-done.8.refs_3_), channel_id=1, source_target_pairs={{0,56},{4,60},{8,0},{12,4},{16,8},{20,12},{24,16},{28,20},{32,24},... | collective-permute-start | bytes 1425416 | tf_op jit(solution)/shard_map/ppermute | solution.py:27
  43.4 2.6 %collective-permute-start.15 = (bf16[64,3712]{1,0:T(8,128)(2,1)S(1)}, bf16[64,3712]{1,0:T(8,128)(2,1)S(1)}, u32[]{:S(2)}, u32[]{:S(2)}) collective-permute-start(bf16[64,3712]{1,0:T(8,128)(2,1)S(1)} %pad_maximum_fusion.3), channel_id=1, source_target_pairs={{0,192},{4,196},{8,200},{12,204},{16,208},{20,212},{24,216},{28,22... | collective-permute-start | bytes 1425416 | tf_op jit(solution)/shard_map/ppermute | solution.py:27
  46.1 4.9 %scores.4 = (f32[8,256]{1,0:T(8,128)S(1)}, f32[8,128]{1,0:T(8,128)S(1)}) custom-call(s32[2]{0:T(128)S(1)} %pad_add_fusion.where, bf16[4,128,3584]{2,1,0:T(8,128)(2,1)S(1)} %constant_dynamic-slice_fusion.q_mine, bf16[4,128,3584]{2,1,0:T(8,128)(2,1)S(1)} %collective-permute-done.11.q_other, bf16[512,256]{1,0:T(8,128)(2,1)S(1)} %pad_maximum_fusion.13.refs_0_, ...), custom_call_target="tpu_custom_call" | custom-call | flops 1879048192 | bytes 9175040 | tf_op jit(solution)/shard_map/scores/pallas_call | solution.py:121
  51.1 0.7 collective-permute-done.13.refs_3_
  51.8 2.4 %collective-permute-done.15.refs_5_ = bf16[64,3712]{1,0:T(8,128)(2,1)S(1)} collective-permute-done((bf16[64,3712]{1,0:T(8,128)(2,1)S(1)}, bf16[64,3712]{1,0:T(8,128)(2,1)S(1)}, u32[]{:S(2)}, u32[]{:S(2)}) %collective-permute-start.15) | collective-permute-done | bytes 475168 | tf_op jit(solution)/shard_map/ppermute | solution.py:27
  54.3 3.1 %collective-permute-done.12.refs_4_ = bf16[64,3712]{1,0:T(8,128)(2,1)S(1)} collective-permute-done((bf16[64,3712]{1,0:T(8,128)(2,1)S(1)}, bf16[64,3712]{1,0:T(8,128)(2,1)S(1)}, u32[]{:S(2)}, u32[]{:S(2)}) %collective-permute-start.12) | collective-permute-done | bytes 475168 | tf_op jit(solution)/shard_map/ppermute | solution.py:27
  57.5 0.4 collective-permute-start.18
  57.8 2.7 %collective-permute-start.20 = (bf16[64,3712]{1,0:T(8,128)(2,1)S(1)}, bf16[64,3712]{1,0:T(8,128)(2,1)S(1)}, u32[]{:S(2)}, u32[]{:S(2)}) collective-permute-start(bf16[64,3712]{1,0:T(8,128)(2,1)S(1)} %pad_maximum_fusion.5), channel_id=1, source_target_pairs={{0,192},{4,196},{8,200},{12,204},{16,208},{20,212},{24,216},{28,22... | collective-permute-start | bytes 1425416 | tf_op jit(solution)/shard_map/ppermute | solution.py:27
  60.5 1.2 collective-permute-start.19
  61.7 4.2 %scores.5 = (f32[8,256]{1,0:T(8,128)S(1)}, f32[8,128]{1,0:T(8,128)S(1)}) custom-call(s32[2]{0:T(128)S(1)} %pad_add_fusion.where, bf16[4,128,3584]{2,1,0:T(8,128)(2,1)S(1)} %constant_dynamic-slice_fusion.q_mine, bf16[4,128,3584]{2,1,0:T(8,128)(2,1)S(1)} %collective-permute-done.11.q_other, bf16[512,256]{1,0:T(8,128)(2,1)S(1)} %pad_maximum_fusion.13.refs_0_, ...), custom_call_target="tpu_custom_call" | custom-call | flops 1879048192 | bytes 9175040 | tf_op jit(solution)/shard_map/scores/pallas_call | solution.py:121
  66.0 2.3 %collective-permute-done.19.refs_2_ = bf16[48,3712]{1,0:T(8,128)(2,1)S(1)} collective-permute-done((bf16[48,3712]{1,0:T(8,128)(2,1)S(1)}, bf16[48,3712]{1,0:T(8,128)(2,1)S(1)}, u32[]{:S(2)}, u32[]{:S(2)}) %collective-permute-start.19) | collective-permute-done | bytes 356384 | tf_op jit(solution)/shard_map/ppermute | solution.py:27
  68.4 0.1 collective-permute-start.21
  68.5 2.7 %collective-permute-start.22 = (bf16[32,3712]{1,0:T(8,128)(2,1)S(1)}, bf16[32,3712]{1,0:T(8,128)(2,1)S(1)}, u32[]{:S(2)}, u32[]{:S(2)}) collective-permute-start(bf16[32,3712]{1,0:T(8,128)(2,1)S(1)} %get-tuple-element.67), channel_id=1, source_target_pairs={{0,192},{4,196},{8,200},{12,204},{16,208},{20,212},{24,216},{28,22... | collective-permute-start | bytes 712712 | tf_op jit(solution)/shard_map/ppermute | solution.py:27
  71.2 0.7 collective-permute-start.23
  71.9 1.9 %collective-permute-start.24 = (bf16[32,3712]{1,0:T(8,128)(2,1)S(1)}, bf16[32,3712]{1,0:T(8,128)(2,1)S(1)}, u32[]{:S(2)}, u32[]{:S(2)}) collective-permute-start(bf16[32,3712]{1,0:T(8,128)(2,1)S(1)} %get-tuple-element.69), channel_id=1, source_target_pairs={{0,56},{4,60},{8,0},{12,4},{16,8},{20,12},{24,16},{28,20},{32,24},... | collective-permute-start | bytes 712712 | tf_op jit(solution)/shard_map/ppermute | solution.py:27
  73.9 4.2 %scores.6 = (f32[8,256]{1,0:T(8,128)S(1)}, f32[8,128]{1,0:T(8,128)S(1)}) custom-call(s32[2]{0:T(128)S(1)} %pad_add_fusion.where, bf16[4,128,3584]{2,1,0:T(8,128)(2,1)S(1)} %constant_dynamic-slice_fusion.q_mine, bf16[4,128,3584]{2,1,0:T(8,128)(2,1)S(1)} %collective-permute-done.11.q_other, bf16[512,256]{1,0:T(8,128)(2,1)S(1)} %pad_maximum_fusion.13.refs_0_, ...), custom_call_target="tpu_custom_call" | custom-call | flops 1879048192 | bytes 9175040 | tf_op jit(solution)/shard_map/scores/pallas_call | solution.py:121
  78.2 5.0 %collective-permute-done.25.refs_8_ = bf16[32,3712]{1,0:T(8,128)(2,1)S(1)} collective-permute-done((bf16[32,3712]{1,0:T(8,128)(2,1)S(1)}, bf16[32,3712]{1,0:T(8,128)(2,1)S(1)}, u32[]{:S(2)}, u32[]{:S(2)}) %collective-permute-start.25) | collective-permute-done | bytes 237600 | tf_op jit(solution)/shard_map/ppermute | solution.py:27
  83.2 4.9 %scores.7 = (f32[8,256]{1,0:T(8,128)S(1)}, f32[8,128]{1,0:T(8,128)S(1)}) custom-call(s32[2]{0:T(128)S(1)} %pad_add_fusion.where, bf16[4,128,3584]{2,1,0:T(8,128)(2,1)S(1)} %constant_dynamic-slice_fusion.q_mine, bf16[4,128,3584]{2,1,0:T(8,128)(2,1)S(1)} %collective-permute-done.11.q_other, bf16[512,256]{1,0:T(8,128)(2,1)S(1)} %pad_maximum_fusion.13.refs_0_, ...), custom_call_target="tpu_custom_call" | custom-call | flops 1879048192 | bytes 9175040 | tf_op jit(solution)/shard_map/scores/pallas_call | solution.py:121
  88.1 0.1 reshape.44
  88.2 0.1 reshape.41
  88.3 0.1 copy.10
  88.4 0.3 fusion.1
  88.8 0.4 all_to_all.8
  89.2 28.0 %all_to_all.10 = f32[256,1,192]{2,1,0:T(1,128)S(1)} all-to-all(f32[256,1,192]{2,1,0:T(1,128)S(1)} %all_to_all.8), channel_id=1, replica_groups=mesh['row'=64,'col'=4] {'row','col'}, dimensions={0} | all-to-all | bytes 393216 | tf_op jit(solution)/shard_map/all_to_all | solution.py:231
  117.2 0.3 reduce_sum.9
  117.5 0.7 reshape.42
  118.2 0.7 reshape.43
  (75 shorter events, 1.2 us)
Async XLA Ops:
  2.4 5.7 %collective-permute-start = (bf16[16,3712]{1,0:T(8,128)(2,1)S(1)}, bf16[16,3712]{1,0:T(8,128)(2,1)S(1)}, u32[]{:S(2)}, u32[]{:S(2)}) collective-permute-start(bf16[16,3712]{1,0:T(8,128)(2,1)S(1)} %pad_maximum_fusion.15), channel_id=1, source_target_pairs={{0,4},{4,0},{8,12},{12,8},{16,20},{20,16},{24,28},{28,24},{32,36},... | collective-permute-start | bytes 356360 | tf_op jit(solution)/shard_map/ppermute | solution.py:31
  5.7 1.5 %collective-permute-start.5 = (bf16[256,128]{1,0:T(8,128)(2,1)}, bf16[256,128]{1,0:T(8,128)(2,1)S(1)}, u32[]{:S(2)}, u32[]{:S(2)}) collective-permute-start(bf16[256,128]{1,0:T(8,128)(2,1)} %param.8), channel_id=1, source_target_pairs={{0,4},{4,0},{8,12},{12,8},{16,20},{20,16},{24,28},{28,24},{32,36},... | collective-permute-start | bytes 196616 | tf_op jit(solution)/shard_map/ppermute | solution.py:31
  8.1 11.8 %collective-permute-start.2 = (bf16[32,3712]{1,0:T(8,128)(2,1)S(1)}, bf16[32,3712]{1,0:T(8,128)(2,1)S(1)}, u32[]{:S(2)}, u32[]{:S(2)}) collective-permute-start(bf16[32,3712]{1,0:T(8,128)(2,1)S(1)} %maximum_select_fusion.refs_2_), channel_id=1, source_target_pairs={{0,8},{4,12},{8,16},{12,20},{16,24},{20,28},{24,32},{28,36},{32,40... | collective-permute-start | bytes 712712 | tf_op jit(solution)/shard_map/ppermute | solution.py:27
  8.2 11.6 %collective-permute-start.3 = (bf16[32,3712]{1,0:T(8,128)(2,1)S(1)}, bf16[32,3712]{1,0:T(8,128)(2,1)S(1)}, u32[]{:S(2)}, u32[]{:S(2)}) collective-permute-start(bf16[32,3712]{1,0:T(8,128)(2,1)S(1)} %maximum_select_fusion.refs_2_), channel_id=1, source_target_pairs={{0,192},{4,196},{8,200},{12,204},{16,208},{20,212},{24,216},{28,22... | collective-permute-start | bytes 712712 | tf_op jit(solution)/shard_map/ppermute | solution.py:27
  10.5 9.3 %collective-permute-start.1 = (bf16[32,3712]{1,0:T(8,128)(2,1)S(1)}, bf16[32,3712]{1,0:T(8,128)(2,1)S(1)}, u32[]{:S(2)}, u32[]{:S(2)}) collective-permute-start(bf16[32,3712]{1,0:T(8,128)(2,1)S(1)} %maximum_select_fusion.refs_2_), channel_id=1, source_target_pairs={{0,64},{4,68},{8,72},{12,76},{16,80},{20,84},{24,88},{28,92},{32,9... | collective-permute-start | bytes 712712 | tf_op jit(solution)/shard_map/ppermute | solution.py:27
  10.5 9.3 %collective-permute-start.4 = (bf16[32,3712]{1,0:T(8,128)(2,1)S(1)}, bf16[32,3712]{1,0:T(8,128)(2,1)S(1)}, u32[]{:S(2)}, u32[]{:S(2)}) collective-permute-start(bf16[32,3712]{1,0:T(8,128)(2,1)S(1)} %maximum_select_fusion.refs_2_), channel_id=1, source_target_pairs={{0,56},{4,60},{8,0},{12,4},{16,8},{20,12},{24,16},{28,20},{32,24},... | collective-permute-start | bytes 712712 | tf_op jit(solution)/shard_map/ppermute | solution.py:27
  14.6 5.2 %collective-permute-start.6 = (bf16[256,256]{1,0:T(8,128)(2,1)S(1)}, bf16[256,256]{1,0:T(8,128)(2,1)S(1)}, u32[]{:S(2)}, u32[]{:S(2)}) collective-permute-start(bf16[256,256]{1,0:T(8,128)(2,1)S(1)} %pad_maximum_fusion.14), channel_id=1, source_target_pairs={{0,3},{1,0},{2,1},{3,2},{4,7},{5,4},{6,5},{7,6},{8,11},{9,8},{10,9... | collective-permute-start | bytes 393224 | tf_op jit(solution)/shard_map/ppermute | solution.py:35
  17.3 9.6 %copy-start = (bf16[4,128,7168]{2,1,0:T(8,128)(2,1)S(1)}, bf16[4,128,7168]{2,1,0:T(8,128)(2,1)}, u32[]{:S(2)}) copy-start(bf16[4,128,7168]{2,1,0:T(8,128)(2,1)} %param.7) | copy-start | bytes 22020100
  20.0 17.8 %collective-permute-start.11 = (bf16[4,128,3584]{2,1,0:T(8,128)(2,1)S(1)}, bf16[4,128,3584]{2,1,0:T(8,128)(2,1)S(1)}, u32[]{:S(2)}, u32[]{:S(2)}) collective-permute-start(bf16[4,128,3584]{2,1,0:T(8,128)(2,1)S(1)} %constant_dynamic-slice_fusion.1), channel_id=1, source_target_pairs={{0,4},{4,0},{8,12},{12,8},{16,20},{20,16},{24,28},{28,24},{32,36},... | collective-permute-start | bytes 11010056 | tf_op jit(solution)/shard_map/ppermute | solution.py:31
  21.4 16.3 %collective-permute-start.8 = (bf16[64,3712]{1,0:T(8,128)(2,1)S(1)}, bf16[64,3712]{1,0:T(8,128)(2,1)S(1)}, u32[]{:S(2)}, u32[]{:S(2)}) collective-permute-start(bf16[64,3712]{1,0:T(8,128)(2,1)S(1)} %pad_maximum_fusion.1), channel_id=1, source_target_pairs={{0,56},{4,60},{8,0},{12,4},{16,8},{20,12},{24,16},{28,20},{32,24},... | collective-permute-start | bytes 1425416 | tf_op jit(solution)/shard_map/ppermute | solution.py:27
  24.3 13.3 %collective-permute-start.9 = (bf16[64,3712]{1,0:T(8,128)(2,1)S(1)}, bf16[64,3712]{1,0:T(8,128)(2,1)S(1)}, u32[]{:S(2)}, u32[]{:S(2)}) collective-permute-start(bf16[64,3712]{1,0:T(8,128)(2,1)S(1)} %pad_maximum_fusion), channel_id=1, source_target_pairs={{0,8},{4,12},{8,16},{12,20},{16,24},{20,28},{24,32},{28,36},{32,40... | collective-permute-start | bytes 1425416 | tf_op jit(solution)/shard_map/ppermute | solution.py:27
  24.3 10.0 %collective-permute-start.10 = (bf16[48,3712]{1,0:T(8,128)(2,1)S(1)}, bf16[48,3712]{1,0:T(8,128)(2,1)S(1)}, u32[]{:S(2)}, u32[]{:S(2)}) collective-permute-start(bf16[48,3712]{1,0:T(8,128)(2,1)S(1)} %pad_maximum_fusion.7), channel_id=1, source_target_pairs={{0,192},{4,196},{8,200},{12,204},{16,208},{20,212},{24,216},{28,22... | collective-permute-start | bytes 1069064 | tf_op jit(solution)/shard_map/ppermute | solution.py:27
  26.9 10.4 %collective-permute-start.7 = (bf16[48,3712]{1,0:T(8,128)(2,1)S(1)}, bf16[48,3712]{1,0:T(8,128)(2,1)S(1)}, u32[]{:S(2)}, u32[]{:S(2)}) collective-permute-start(bf16[48,3712]{1,0:T(8,128)(2,1)S(1)} %pad_maximum_fusion.6), channel_id=1, source_target_pairs={{0,64},{4,68},{8,72},{12,76},{16,80},{20,84},{24,88},{28,92},{32,9... | collective-permute-start | bytes 1069064 | tf_op jit(solution)/shard_map/ppermute | solution.py:27
  37.8 13.2 %collective-permute-start.14 = (bf16[64,3712]{1,0:T(8,128)(2,1)S(1)}, bf16[64,3712]{1,0:T(8,128)(2,1)S(1)}, u32[]{:S(2)}, u32[]{:S(2)}) collective-permute-start(bf16[64,3712]{1,0:T(8,128)(2,1)S(1)} %collective-permute-done.9.refs_2_), channel_id=1, source_target_pairs={{0,8},{4,12},{8,16},{12,20},{16,24},{20,28},{24,32},{28,36},{32,40... | collective-permute-start | bytes 1425416 | tf_op jit(solution)/shard_map/ppermute | solution.py:27
  37.9 8.2 %collective-permute-start.16 = (bf16[512,256]{1,0:T(8,128)(2,1)S(1)}, bf16[512,256]{1,0:T(8,128)(2,1)S(1)}, u32[]{:S(2)}, u32[]{:S(2)}) collective-permute-start(bf16[512,256]{1,0:T(8,128)(2,1)S(1)} %pad_maximum_fusion.13.refs_0_), channel_id=1, source_target_pairs={{0,2},{1,3},{2,0},{3,1},{4,6},{5,7},{6,4},{7,5},{8,10},{9,11},{10,... | collective-permute-start | bytes 786440 | tf_op jit(solution)/shard_map/ppermute | solution.py:35
  40.9 10.9 %collective-permute-start.13 = (bf16[64,3712]{1,0:T(8,128)(2,1)S(1)}, bf16[64,3712]{1,0:T(8,128)(2,1)S(1)}, u32[]{:S(2)}, u32[]{:S(2)}) collective-permute-start(bf16[64,3712]{1,0:T(8,128)(2,1)S(1)} %collective-permute-done.8.refs_3_), channel_id=1, source_target_pairs={{0,56},{4,60},{8,0},{12,4},{16,8},{20,12},{24,16},{28,20},{32,24},... | collective-permute-start | bytes 1425416 | tf_op jit(solution)/shard_map/ppermute | solution.py:27
  43.4 10.7 %collective-permute-start.15 = (bf16[64,3712]{1,0:T(8,128)(2,1)S(1)}, bf16[64,3712]{1,0:T(8,128)(2,1)S(1)}, u32[]{:S(2)}, u32[]{:S(2)}) collective-permute-start(bf16[64,3712]{1,0:T(8,128)(2,1)S(1)} %pad_maximum_fusion.3), channel_id=1, source_target_pairs={{0,192},{4,196},{8,200},{12,204},{16,208},{20,212},{24,216},{28,22... | collective-permute-start | bytes 1425416 | tf_op jit(solution)/shard_map/ppermute | solution.py:27
  46.0 11.3 %collective-permute-start.12 = (bf16[64,3712]{1,0:T(8,128)(2,1)S(1)}, bf16[64,3712]{1,0:T(8,128)(2,1)S(1)}, u32[]{:S(2)}, u32[]{:S(2)}) collective-permute-start(bf16[64,3712]{1,0:T(8,128)(2,1)S(1)} %pad_maximum_fusion.2), channel_id=1, source_target_pairs={{0,64},{4,68},{8,72},{12,76},{16,80},{20,84},{24,88},{28,92},{32,9... | collective-permute-start | bytes 1425416 | tf_op jit(solution)/shard_map/ppermute | solution.py:27
  57.4 16.4 %copy-start.1 = (s32[64]{0:T(128)S(1)}, s32[64]{0:T(128)}, u32[]{:S(2)}) copy-start(s32[64]{0:T(128)} %constant.51.clone) | copy-start | bytes 772
  57.4 16.4 %copy-start.2 = (s32[64]{0:T(128)S(1)}, s32[64]{0:T(128)}, u32[]{:S(2)}) copy-start(s32[64]{0:T(128)} %constant.52.clone) | copy-start | bytes 772
  57.4 16.4 %copy-start.3 = (s32[64]{0:T(128)S(1)}, s32[64]{0:T(128)}, u32[]{:S(2)}) copy-start(s32[64]{0:T(128)} %constant.53.clone) | copy-start | bytes 772
  57.5 8.5 %collective-permute-start.18 = (bf16[48,3712]{1,0:T(8,128)(2,1)S(1)}, bf16[48,3712]{1,0:T(8,128)(2,1)S(1)}, u32[]{:S(2)}, u32[]{:S(2)}) collective-permute-start(bf16[48,3712]{1,0:T(8,128)(2,1)S(1)} %slice.170), channel_id=1, source_target_pairs={{0,56},{4,60},{8,0},{12,4},{16,8},{20,12},{24,16},{28,20},{32,24},... | collective-permute-start | bytes 1069064 | tf_op jit(solution)/shard_map/ppermute | solution.py:27
  57.8 10.5 %collective-permute-start.17 = (bf16[64,3712]{1,0:T(8,128)(2,1)S(1)}, bf16[64,3712]{1,0:T(8,128)(2,1)S(1)}, u32[]{:S(2)}, u32[]{:S(2)}) collective-permute-start(bf16[64,3712]{1,0:T(8,128)(2,1)S(1)} %pad_maximum_fusion.4), channel_id=1, source_target_pairs={{0,64},{4,68},{8,72},{12,76},{16,80},{20,84},{24,88},{28,92},{32,9... | collective-permute-start | bytes 1425416 | tf_op jit(solution)/shard_map/ppermute | solution.py:27
  57.8 10.4 %collective-permute-start.20 = (bf16[64,3712]{1,0:T(8,128)(2,1)S(1)}, bf16[64,3712]{1,0:T(8,128)(2,1)S(1)}, u32[]{:S(2)}, u32[]{:S(2)}) collective-permute-start(bf16[64,3712]{1,0:T(8,128)(2,1)S(1)} %pad_maximum_fusion.5), channel_id=1, source_target_pairs={{0,192},{4,196},{8,200},{12,204},{16,208},{20,212},{24,216},{28,22... | collective-permute-start | bytes 1425416 | tf_op jit(solution)/shard_map/ppermute | solution.py:27
  60.5 7.7 %collective-permute-start.19 = (bf16[48,3712]{1,0:T(8,128)(2,1)S(1)}, bf16[48,3712]{1,0:T(8,128)(2,1)S(1)}, u32[]{:S(2)}, u32[]{:S(2)}) collective-permute-start(bf16[48,3712]{1,0:T(8,128)(2,1)S(1)} %pad_maximum_fusion.8), channel_id=1, source_target_pairs={{0,8},{4,12},{8,16},{12,20},{16,24},{20,28},{24,32},{28,36},{32,40... | collective-permute-start | bytes 1069064 | tf_op jit(solution)/shard_map/ppermute | solution.py:27
  68.4 9.7 %collective-permute-start.21 = (bf16[32,3712]{1,0:T(8,128)(2,1)S(1)}, bf16[32,3712]{1,0:T(8,128)(2,1)S(1)}, u32[]{:S(2)}, u32[]{:S(2)}) collective-permute-start(bf16[32,3712]{1,0:T(8,128)(2,1)S(1)} %get-tuple-element.66), channel_id=1, source_target_pairs={{0,64},{4,68},{8,72},{12,76},{16,80},{20,84},{24,88},{28,92},{32,9... | collective-permute-start | bytes 712712 | tf_op jit(solution)/shard_map/ppermute | solution.py:27
  68.5 9.7 %collective-permute-start.22 = (bf16[32,3712]{1,0:T(8,128)(2,1)S(1)}, bf16[32,3712]{1,0:T(8,128)(2,1)S(1)}, u32[]{:S(2)}, u32[]{:S(2)}) collective-permute-start(bf16[32,3712]{1,0:T(8,128)(2,1)S(1)} %get-tuple-element.67), channel_id=1, source_target_pairs={{0,192},{4,196},{8,200},{12,204},{16,208},{20,212},{24,216},{28,22... | collective-permute-start | bytes 712712 | tf_op jit(solution)/shard_map/ppermute | solution.py:27
  71.2 7.0 %collective-permute-start.23 = (bf16[32,3712]{1,0:T(8,128)(2,1)S(1)}, bf16[32,3712]{1,0:T(8,128)(2,1)S(1)}, u32[]{:S(2)}, u32[]{:S(2)}) collective-permute-start(bf16[32,3712]{1,0:T(8,128)(2,1)S(1)} %get-tuple-element.68), channel_id=1, source_target_pairs={{0,8},{4,12},{8,16},{12,20},{16,24},{20,28},{24,32},{28,36},{32,40... | collective-permute-start | bytes 712712 | tf_op jit(solution)/shard_map/ppermute | solution.py:27
  71.9 6.3 %collective-permute-start.24 = (bf16[32,3712]{1,0:T(8,128)(2,1)S(1)}, bf16[32,3712]{1,0:T(8,128)(2,1)S(1)}, u32[]{:S(2)}, u32[]{:S(2)}) collective-permute-start(bf16[32,3712]{1,0:T(8,128)(2,1)S(1)} %get-tuple-element.69), channel_id=1, source_target_pairs={{0,56},{4,60},{8,0},{12,4},{16,8},{20,12},{24,16},{28,20},{32,24},... | collective-permute-start | bytes 712712 | tf_op jit(solution)/shard_map/ppermute | solution.py:27
  73.9 9.3 %collective-permute-start.25 = (bf16[32,3712]{1,0:T(8,128)(2,1)S(1)}, bf16[32,3712]{1,0:T(8,128)(2,1)S(1)}, u32[]{:S(2)}, u32[]{:S(2)}) collective-permute-start(bf16[32,3712]{1,0:T(8,128)(2,1)S(1)} %concatenate.107), channel_id=1, source_target_pairs={{0,72},{4,76},{8,80},{12,84},{16,88},{20,92},{24,96},{28,100},{32,... | collective-permute-start | bytes 712712 | tf_op jit(solution)/shard_map/ppermute | solution.py:27
where the time goes:
time: 119 us
  starting transfers between devices  37.4 us (31%)
  blocking collectives  28 us (24%)
  waiting for transfers between devices  25.1 us (21%)
  Pallas kernels  18.3 us (15%)
  local copies, waits for them, and re-layouts  6.17 us (5%)
  other arithmetic  2.47 us (2%)
    all_to_all x1, blocking collectives, body(): arrived = lax.all_to_all(parts, ('row', 'col'), 0, 0, tiled=True)  28 us
    ppermute x21, starting transfers between devices, shift(): return lax.ppermute(block, 'row', pairs)  26.9 us
    ppermute x21, waiting for transfers between devices, shift(): return lax.ppermute(block, 'row', pairs)  23.8 us
    pallas_call x4, Pallas kernels, piece_scores(): pl.pallas_call(functools.partial(scores_kernel, places, sizes), out_shape...  18.3 us
    ppermute x2, starting transfers between devices, from_col(): lax.ppermute(block, 'col', [(i, (i - ahead) % cols) for i in range(cols)])  5.73 us
    ppermute x3, starting transfers between devices, swap(): return lax.ppermute(block, 'row', [(i, i ^ 1) for i in range(NX * NZ * 2)])  4.78 us
    dynamic_slice x3, local copies, waits for them, and re-layouts, columns(): return lax.dynamic_slice(array, start, array.shape[:-1] + (half,))  3.63 us
  transfers between devices with their start and end apart: 26, of which 9 were waited for; matrix products, arithmetic and copies ran while one was open for 3% of the time, Pallas kernels for 11%

commit v1 on v0

--- a/solution.py
+++ b/solution.py
@@ -159,14 +159,14 @@
         start = (0,) * (array.ndim - 1) + (which * half,)
         return lax.dynamic_slice(array, start, array.shape[:-1] + (half,))
 
-    ids = jnp.broadcast_to(seq_ids[:, None].astype(activations.dtype), (tokens, 128))
+    ids = jnp.broadcast_to(seq_ids[:, None], (tokens, 128)).astype(activations.dtype)
     mine = cat([columns(activations, core), ids], 1)
     other = swap(cat([columns(activations, 1 - core), ids], 1))
     own = jnp.where(core == 0, cat([mine, other]), cat([other, mine]))
 
     own, where, query_grads = lax.optimization_barrier((own, where, query_grads))
 
-    q_other = columns(query_grads, 1 - core)
+    q_slice = columns(query_grads, 1 - core)
     slices = cat([out_grads, swap(out_grads)], 1)
     slices, _ = lax.optimization_barrier((slices, own))
     slices = cat([slices, from_col(slices, 1, cols)])
@@ -190,18 +190,21 @@
     for number, moves in enumerate(ROUNDS):
         sent = [cat([cat([held[src, h] for h in part]) for src, part, _ in load]) for _, load in moves]
         if number == 1:
-            sent, slices, q_other, query_grads = lax.optimization_barrier(
-                (sent, slices, q_other, query_grads)
+            sent, slices, q_slice, query_grads = lax.optimization_barrier(
+                (sent, slices, q_slice, query_grads)
             )
-            q_other, q_mine = swap(q_other), columns(query_grads, core)
+            slices, q_mine = [slices, from_col(slices, 2, cols)], columns(query_grads, core)
         if number == 2:
-            sent, slices, q_other, q_mine = lax.optimization_barrier(
-                (sent, slices, q_other, q_mine)
+            sent, slices, q_slice, q_mine = lax.optimization_barrier(
+                (sent, slices, q_slice, q_mine)
             )
-            slices = [slices, from_col(slices, 2, cols)]
-        if number > 2:
-            sent, scores[-1] = lax.optimization_barrier((sent, scores[-1]))
-        if number > 1:
+            q_other = swap(q_slice)
+        if number == 3:
+            sent, slices, q_other = lax.optimization_barrier((sent, slices, q_other))
+            work()
+            work()
+        if number == 4:
+            sent, scores = lax.optimization_barrier((sent, scores))
             work()
         for ((dx, dz), load), block in zip(moves, sent):
             came = shift(block, dx, dz)

time: 119 us -> 115 us (0.966)
  waiting for transfers between devices: 25.1 us -> 20 us
  starting transfers between devices: 37.4 us -> 39.2 us
    ppermute x21, waiting for transfers between devices: 23.8 us -> 18 us  [shift(): return lax.ppermute(block, 'row', pairs)]
    ppermute x3, starting transfers between devices: 4.78 us -> 7.27 us  [swap(): return lax.ppermute(block, 'row', [(i, i ^ 1) for i in range(NX * NZ * 2)])]
  transfers between devices with their start and end apart: 26 -> 26, of which waited for: 9 -> 10; matrix products, arithmetic and copies ran while one was open for 3% -> 4% of each run, Pallas kernels for 11% -> 12%
where the time goes in v1:
time: 115 us
  starting transfers between devices  39.2 us (34%)
  blocking collectives  27.5 us (24%)
  waiting for transfers between devices  20 us (17%)
  Pallas kernels  18.3 us (16%)
  local copies, waits for them, and re-layouts  6.17 us (5%)
  other arithmetic  2.46 us (2%)
    all_to_all x1, blocking collectives, body(): arrived = lax.all_to_all(parts, ('row', 'col'), 0, 0, tiled=True)  27.5 us
    ppermute x21, starting transfers between devices, shift(): return lax.ppermute(block, 'row', pairs)  26.3 us
    pallas_call x4, Pallas kernels, piece_scores(): pl.pallas_call(functools.partial(scores_kernel, places, sizes), out_shape...  18.3 us
    ppermute x21, waiting for transfers between devices, shift(): return lax.ppermute(block, 'row', pairs)  18 us
    ppermute x3, starting transfers between devices, swap(): return lax.ppermute(block, 'row', [(i, i ^ 1) for i in range(NX * NZ * 2)])  7.27 us
    ppermute x2, starting transfers between devices, from_col(): lax.ppermute(block, 'col', [(i, (i - ahead) % cols) for i in range(cols)])  5.65 us
    dynamic_slice x3, local copies, waits for them, and re-layouts, columns(): return lax.dynamic_slice(array, start, array.shape[:-1] + (half,))  3.63 us
  transfers between devices with their start and end apart: 26, of which 10 were waited for; matrix products, arithmetic and copies ran while one was open for 4% of the time, Pallas kernels for 12%

profile of v1, /device:TPU:1, one launch (start us, length us, event | category | flops | bytes accessed | tf_op | source)
XLA Modules:
  0.0 115.0 jit_solution(13806694460016720830)
XLA Ops:
  0.6 0.7 convert_element_type.5
  1.3 1.0 constant_dynamic-slice_fusion.3
  2.4 3.3 %collective-permute-start = (bf16[16,3712]{1,0:T(8,128)(2,1)S(1)}, bf16[16,3712]{1,0:T(8,128)(2,1)S(1)}, u32[]{:S(2)}, u32[]{:S(2)}) collective-permute-start(bf16[16,3712]{1,0:T(8,128)(2,1)S(1)} %pad_maximum_fusion.15), channel_id=1, source_target_pairs={{0,4},{4,0},{8,12},{12,8},{16,20},{20,16},{24,28},{28,24},{32,36},... | collective-permute-start | bytes 356360 | tf_op jit(solution)/shard_map/ppermute | solution.py:31
  5.7 0.1 collective-permute-start.5
  5.8 0.1 pad_add_fusion.where
  5.9 1.3 %collective-permute-done.5 = bf16[256,128]{1,0:T(8,128)(2,1)S(1)} collective-permute-done((bf16[256,128]{1,0:T(8,128)(2,1)}, bf16[256,128]{1,0:T(8,128)(2,1)S(1)}, u32[]{:S(2)}, u32[]{:S(2)}) %collective-permute-start.5) | collective-permute-done | bytes 65568 | tf_op jit(solution)/shard_map/ppermute | solution.py:31
  7.2 0.9 pad_maximum_fusion.14
  8.1 0.1 collective-permute-start.2
  8.2 2.4 %collective-permute-start.3 = (bf16[32,3712]{1,0:T(8,128)(2,1)S(1)}, bf16[32,3712]{1,0:T(8,128)(2,1)S(1)}, u32[]{:S(2)}, u32[]{:S(2)}) collective-permute-start(bf16[32,3712]{1,0:T(8,128)(2,1)S(1)} %maximum_select_fusion.refs_2_), channel_id=1, source_target_pairs={{0,192},{4,196},{8,200},{12,204},{16,208},{20,212},{24,216},{28,22... | collective-permute-start | bytes 712712 | tf_op jit(solution)/shard_map/ppermute | solution.py:27
  10.5 4.0 %collective-permute-start.4 = (bf16[32,3712]{1,0:T(8,128)(2,1)S(1)}, bf16[32,3712]{1,0:T(8,128)(2,1)S(1)}, u32[]{:S(2)}, u32[]{:S(2)}) collective-permute-start(bf16[32,3712]{1,0:T(8,128)(2,1)S(1)} %maximum_select_fusion.refs_2_), channel_id=1, source_target_pairs={{0,56},{4,60},{8,0},{12,4},{16,8},{20,12},{24,16},{28,20},{32,24},... | collective-permute-start | bytes 712712 | tf_op jit(solution)/shard_map/ppermute | solution.py:27
  14.6 2.7 %collective-permute-start.6 = (bf16[256,256]{1,0:T(8,128)(2,1)S(1)}, bf16[256,256]{1,0:T(8,128)(2,1)S(1)}, u32[]{:S(2)}, u32[]{:S(2)}) collective-permute-start(bf16[256,256]{1,0:T(8,128)(2,1)S(1)} %pad_maximum_fusion.14), channel_id=1, source_target_pairs={{0,3},{1,0},{2,1},{3,2},{4,7},{5,4},{6,5},{7,6},{8,11},{9,8},{10,9... | collective-permute-start | bytes 393224 | tf_op jit(solution)/shard_map/ppermute | solution.py:35
  17.3 2.4 %constant_dynamic-slice_fusion.1 = bf16[4,128,3584]{2,1,0:T(8,128)(2,1)S(1)} fusion(bf16[4,128,7168]{2,1,0:T(8,128)(2,1)} %param.7, s32[]{:T(128)S(6)} %select_n.18), kind=kLoop, calls=%fused_computation.31 | loop fusion | bytes 7340036 | tf_op jit(solution)/shard_map/dynamic_slice | solution.py:160
  20.0 2.9 %collective-permute-start.8 = (bf16[64,3712]{1,0:T(8,128)(2,1)S(1)}, bf16[64,3712]{1,0:T(8,128)(2,1)S(1)}, u32[]{:S(2)}, u32[]{:S(2)}) collective-permute-start(bf16[64,3712]{1,0:T(8,128)(2,1)S(1)} %pad_maximum_fusion.1), channel_id=1, source_target_pairs={{0,56},{4,60},{8,0},{12,4},{16,8},{20,12},{24,16},{28,20},{32,24},... | collective-permute-start | bytes 1425416 | tf_op jit(solution)/shard_map/ppermute | solution.py:27
  23.0 2.3 %collective-permute-start.10 = (bf16[48,3712]{1,0:T(8,128)(2,1)S(1)}, bf16[48,3712]{1,0:T(8,128)(2,1)S(1)}, u32[]{:S(2)}, u32[]{:S(2)}) collective-permute-start(bf16[48,3712]{1,0:T(8,128)(2,1)S(1)} %pad_maximum_fusion.7), channel_id=1, source_target_pairs={{0,192},{4,196},{8,200},{12,204},{16,208},{20,212},{24,216},{28,22... | collective-permute-start | bytes 1069064 | tf_op jit(solution)/shard_map/ppermute | solution.py:27
  25.2 2.9 %collective-permute-start.11 = (bf16[512,256]{1,0:T(8,128)(2,1)S(1)}, bf16[512,256]{1,0:T(8,128)(2,1)S(1)}, u32[]{:S(2)}, u32[]{:S(2)}) collective-permute-start(bf16[512,256]{1,0:T(8,128)(2,1)S(1)} %pad_maximum_fusion.13.refs_0_), channel_id=1, source_target_pairs={{0,2},{1,3},{2,0},{3,1},{4,6},{5,7},{6,4},{7,5},{8,10},{9,11},{10,... | collective-permute-start | bytes 786440 | tf_op jit(solution)/shard_map/ppermute | solution.py:35
  28.2 0.2 constant_dynamic-slice_fusion.q_mine
  28.4 2.8 %collective-permute-done.10.refs_8_ = bf16[48,3712]{1,0:T(8,128)(2,1)S(1)} collective-permute-done((bf16[48,3712]{1,0:T(8,128)(2,1)S(1)}, bf16[48,3712]{1,0:T(8,128)(2,1)S(1)}, u32[]{:S(2)}, u32[]{:S(2)}) %collective-permute-start.10) | collective-permute-done | bytes 356384 | tf_op jit(solution)/shard_map/ppermute | solution.py:27
  31.2 2.9 %collective-permute-done.7.refs_7_ = bf16[48,3712]{1,0:T(8,128)(2,1)S(1)} collective-permute-done((bf16[48,3712]{1,0:T(8,128)(2,1)S(1)}, bf16[48,3712]{1,0:T(8,128)(2,1)S(1)}, u32[]{:S(2)}, u32[]{:S(2)}) %collective-permute-start.7) | collective-permute-done | bytes 356384 | tf_op jit(solution)/shard_map/ppermute | solution.py:27
  34.1 0.8 collective-permute-done.9.refs_2_
  35.1 1.7 %collective-permute-start.13 = (bf16[64,3712]{1,0:T(8,128)(2,1)S(1)}, bf16[64,3712]{1,0:T(8,128)(2,1)S(1)}, u32[]{:S(2)}, u32[]{:S(2)}) collective-permute-start(bf16[64,3712]{1,0:T(8,128)(2,1)S(1)} %collective-permute-done.8.refs_3_), channel_id=1, source_target_pairs={{0,56},{4,60},{8,0},{12,4},{16,8},{20,12},{24,16},{28,20},{32,24},... | collective-permute-start | bytes 1425416 | tf_op jit(solution)/shard_map/ppermute | solution.py:27
  36.8 0.7 collective-permute-start.15
  37.5 0.8 collective-permute-start.12
  38.3 0.4 collective-permute-start.14
  38.6 3.8 %collective-permute-start.16 = (bf16[4,128,3584]{2,1,0:T(8,128)(2,1)S(1)}, bf16[4,128,3584]{2,1,0:T(8,128)(2,1)S(1)}, u32[]{:S(2)}, u32[]{:S(2)}) collective-permute-start(bf16[4,128,3584]{2,1,0:T(8,128)(2,1)S(1)} %constant_dynamic-slice_fusion.1), channel_id=1, source_target_pairs={{0,4},{4,0},{8,12},{12,8},{16,20},{20,16},{24,28},{28,24},{32,36},... | collective-permute-start | bytes 11010056 | tf_op jit(solution)/shard_map/ppermute | solution.py:31
  42.5 2.6 %collective-permute-done.13.refs_3_ = bf16[64,3712]{1,0:T(8,128)(2,1)S(1)} collective-permute-done((bf16[64,3712]{1,0:T(8,128)(2,1)S(1)}, bf16[64,3712]{1,0:T(8,128)(2,1)S(1)}, u32[]{:S(2)}, u32[]{:S(2)}) %collective-permute-start.13) | collective-permute-done | bytes 475168 | tf_op jit(solution)/shard_map/ppermute | solution.py:27
  45.1 0.4 collective-permute-done.15.refs_5_
  45.5 1.2 %collective-permute-done.12.refs_4_ = bf16[64,3712]{1,0:T(8,128)(2,1)S(1)} collective-permute-done((bf16[64,3712]{1,0:T(8,128)(2,1)S(1)}, bf16[64,3712]{1,0:T(8,128)(2,1)S(1)}, u32[]{:S(2)}, u32[]{:S(2)}) %collective-permute-start.12) | collective-permute-done | bytes 475168 | tf_op jit(solution)/shard_map/ppermute | solution.py:27
  46.8 0.9 collective-permute-done.14.refs_2_
  47.8 0.7 collective-permute-done.16.q_other
  48.5 3.0 %collective-permute-start.18 = (bf16[48,3712]{1,0:T(8,128)(2,1)S(1)}, bf16[48,3712]{1,0:T(8,128)(2,1)S(1)}, u32[]{:S(2)}, u32[]{:S(2)}) collective-permute-start(bf16[48,3712]{1,0:T(8,128)(2,1)S(1)} %slice.170), channel_id=1, source_target_pairs={{0,56},{4,60},{8,0},{12,4},{16,8},{20,12},{24,16},{28,20},{32,24},... | collective-permute-start | bytes 1069064 | tf_op jit(solution)/shard_map/ppermute | solution.py:27
  51.5 2.7 %collective-permute-start.20 = (bf16[64,3712]{1,0:T(8,128)(2,1)S(1)}, bf16[64,3712]{1,0:T(8,128)(2,1)S(1)}, u32[]{:S(2)}, u32[]{:S(2)}) collective-permute-start(bf16[64,3712]{1,0:T(8,128)(2,1)S(1)} %pad_maximum_fusion.5), channel_id=1, source_target_pairs={{0,192},{4,196},{8,200},{12,204},{16,208},{20,212},{24,216},{28,22... | collective-permute-start | bytes 1425416 | tf_op jit(solution)/shard_map/ppermute | solution.py:27
  54.1 4.2 %scores.5 = (f32[8,256]{1,0:T(8,128)S(1)}, f32[8,128]{1,0:T(8,128)S(1)}) custom-call(s32[2]{0:T(128)S(1)} %pad_add_fusion.where, bf16[4,128,3584]{2,1,0:T(8,128)(2,1)S(1)} %constant_dynamic-slice_fusion.q_mine, bf16[4,128,3584]{2,1,0:T(8,128)(2,1)S(1)} %collective-permute-done.16.q_other, bf16[512,256]{1,0:T(8,128)(2,1)S(1)} %pad_maximum_fusion.13.refs_0_, ...), custom_call_target="tpu_custom_call" | custom-call | flops 1879048192 | bytes 9175040 | tf_op jit(solution)/shard_map/scores/pallas_call | solution.py:121
  58.4 4.9 %scores.4 = (f32[8,256]{1,0:T(8,128)S(1)}, f32[8,128]{1,0:T(8,128)S(1)}) custom-call(s32[2]{0:T(128)S(1)} %pad_add_fusion.where, bf16[4,128,3584]{2,1,0:T(8,128)(2,1)S(1)} %constant_dynamic-slice_fusion.q_mine, bf16[4,128,3584]{2,1,0:T(8,128)(2,1)S(1)} %collective-permute-done.16.q_other, bf16[512,256]{1,0:T(8,128)(2,1)S(1)} %pad_maximum_fusion.13.refs_0_, ...), custom_call_target="tpu_custom_call" | custom-call | flops 1879048192 | bytes 9175040 | tf_op jit(solution)/shard_map/scores/pallas_call | solution.py:121
  63.6 0.8 collective-permute-start.21
  64.4 2.0 %collective-permute-start.22 = (bf16[32,3712]{1,0:T(8,128)(2,1)S(1)}, bf16[32,3712]{1,0:T(8,128)(2,1)S(1)}, u32[]{:S(2)}, u32[]{:S(2)}) collective-permute-start(bf16[32,3712]{1,0:T(8,128)(2,1)S(1)} %get-tuple-element.75), channel_id=1, source_target_pairs={{0,192},{4,196},{8,200},{12,204},{16,208},{20,212},{24,216},{28,22... | collective-permute-start | bytes 712712 | tf_op jit(solution)/shard_map/ppermute | solution.py:27
  66.3 2.7 %collective-permute-start.24 = (bf16[32,3712]{1,0:T(8,128)(2,1)S(1)}, bf16[32,3712]{1,0:T(8,128)(2,1)S(1)}, u32[]{:S(2)}, u32[]{:S(2)}) collective-permute-start(bf16[32,3712]{1,0:T(8,128)(2,1)S(1)} %get-tuple-element.77), channel_id=1, source_target_pairs={{0,56},{4,60},{8,0},{12,4},{16,8},{20,12},{24,16},{28,20},{32,24},... | collective-permute-start | bytes 712712 | tf_op jit(solution)/shard_map/ppermute | solution.py:27
  69.1 4.2 %scores.6 = (f32[8,256]{1,0:T(8,128)S(1)}, f32[8,128]{1,0:T(8,128)S(1)}) custom-call(s32[2]{0:T(128)S(1)} %pad_add_fusion.where, bf16[4,128,3584]{2,1,0:T(8,128)(2,1)S(1)} %constant_dynamic-slice_fusion.q_mine, bf16[4,128,3584]{2,1,0:T(8,128)(2,1)S(1)} %collective-permute-done.16.q_other, bf16[512,256]{1,0:T(8,128)(2,1)S(1)} %pad_maximum_fusion.13.refs_0_, ...), custom_call_target="tpu_custom_call" | custom-call | flops 1879048192 | bytes 9175040 | tf_op jit(solution)/shard_map/scores/pallas_call | solution.py:121
  73.4 6.4 %collective-permute-done.25.refs_8_ = bf16[32,3712]{1,0:T(8,128)(2,1)S(1)} collective-permute-done((bf16[32,3712]{1,0:T(8,128)(2,1)S(1)}, bf16[32,3712]{1,0:T(8,128)(2,1)S(1)}, u32[]{:S(2)}, u32[]{:S(2)}) %collective-permute-start.25) | collective-permute-done | bytes 237600 | tf_op jit(solution)/shard_map/ppermute | solution.py:27
  79.8 4.9 %scores.7 = (f32[8,256]{1,0:T(8,128)S(1)}, f32[8,128]{1,0:T(8,128)S(1)}) custom-call(s32[2]{0:T(128)S(1)} %pad_add_fusion.where, bf16[4,128,3584]{2,1,0:T(8,128)(2,1)S(1)} %constant_dynamic-slice_fusion.q_mine, bf16[4,128,3584]{2,1,0:T(8,128)(2,1)S(1)} %collective-permute-done.16.q_other, bf16[512,256]{1,0:T(8,128)(2,1)S(1)} %pad_maximum_fusion.13.refs_0_, ...), custom_call_target="tpu_custom_call" | custom-call | flops 1879048192 | bytes 9175040 | tf_op jit(solution)/shard_map/scores/pallas_call | solution.py:121
  84.7 0.1 reshape.43
  84.8 0.1 reshape.40
  84.9 0.1 copy.10
  85.1 0.3 fusion.1
  85.4 0.4 all_to_all.8
  85.8 27.5 %all_to_all.10 = f32[256,1,192]{2,1,0:T(1,128)S(1)} all-to-all(f32[256,1,192]{2,1,0:T(1,128)S(1)} %all_to_all.8), channel_id=1, replica_groups=mesh['row'=64,'col'=4] {'row','col'}, dimensions={0} | all-to-all | bytes 393216 | tf_op jit(solution)/shard_map/all_to_all | solution.py:234
  113.4 0.3 reduce_sum.9
  113.7 0.7 reshape.41
  114.4 0.7 reshape.42
  (75 shorter events, 1.2 us)
Async XLA Ops:
  2.4 5.7 %collective-permute-start = (bf16[16,3712]{1,0:T(8,128)(2,1)S(1)}, bf16[16,3712]{1,0:T(8,128)(2,1)S(1)}, u32[]{:S(2)}, u32[]{:S(2)}) collective-permute-start(bf16[16,3712]{1,0:T(8,128)(2,1)S(1)} %pad_maximum_fusion.15), channel_id=1, source_target_pairs={{0,4},{4,0},{8,12},{12,8},{16,20},{20,16},{24,28},{28,24},{32,36},... | collective-permute-start | bytes 356360 | tf_op jit(solution)/shard_map/ppermute | solution.py:31
  5.7 1.5 %collective-permute-start.5 = (bf16[256,128]{1,0:T(8,128)(2,1)}, bf16[256,128]{1,0:T(8,128)(2,1)S(1)}, u32[]{:S(2)}, u32[]{:S(2)}) collective-permute-start(bf16[256,128]{1,0:T(8,128)(2,1)} %param.8), channel_id=1, source_target_pairs={{0,4},{4,0},{8,12},{12,8},{16,20},{20,16},{24,28},{28,24},{32,36},... | collective-permute-start | bytes 196616 | tf_op jit(solution)/shard_map/ppermute | solution.py:31
  8.1 11.8 %collective-permute-start.2 = (bf16[32,3712]{1,0:T(8,128)(2,1)S(1)}, bf16[32,3712]{1,0:T(8,128)(2,1)S(1)}, u32[]{:S(2)}, u32[]{:S(2)}) collective-permute-start(bf16[32,3712]{1,0:T(8,128)(2,1)S(1)} %maximum_select_fusion.refs_2_), channel_id=1, source_target_pairs={{0,8},{4,12},{8,16},{12,20},{16,24},{20,28},{24,32},{28,36},{32,40... | collective-permute-start | bytes 712712 | tf_op jit(solution)/shard_map/ppermute | solution.py:27
  8.2 11.6 %collective-permute-start.3 = (bf16[32,3712]{1,0:T(8,128)(2,1)S(1)}, bf16[32,3712]{1,0:T(8,128)(2,1)S(1)}, u32[]{:S(2)}, u32[]{:S(2)}) collective-permute-start(bf16[32,3712]{1,0:T(8,128)(2,1)S(1)} %maximum_select_fusion.refs_2_), channel_id=1, source_target_pairs={{0,192},{4,196},{8,200},{12,204},{16,208},{20,212},{24,216},{28,22... | collective-permute-start | bytes 712712 | tf_op jit(solution)/shard_map/ppermute | solution.py:27
  10.5 9.3 %collective-permute-start.1 = (bf16[32,3712]{1,0:T(8,128)(2,1)S(1)}, bf16[32,3712]{1,0:T(8,128)(2,1)S(1)}, u32[]{:S(2)}, u32[]{:S(2)}) collective-permute-start(bf16[32,3712]{1,0:T(8,128)(2,1)S(1)} %maximum_select_fusion.refs_2_), channel_id=1, source_target_pairs={{0,64},{4,68},{8,72},{12,76},{16,80},{20,84},{24,88},{28,92},{32,9... | collective-permute-start | bytes 712712 | tf_op jit(solution)/shard_map/ppermute | solution.py:27
  10.5 9.3 %collective-permute-start.4 = (bf16[32,3712]{1,0:T(8,128)(2,1)S(1)}, bf16[32,3712]{1,0:T(8,128)(2,1)S(1)}, u32[]{:S(2)}, u32[]{:S(2)}) collective-permute-start(bf16[32,3712]{1,0:T(8,128)(2,1)S(1)} %maximum_select_fusion.refs_2_), channel_id=1, source_target_pairs={{0,56},{4,60},{8,0},{12,4},{16,8},{20,12},{24,16},{28,20},{32,24},... | collective-permute-start | bytes 712712 | tf_op jit(solution)/shard_map/ppermute | solution.py:27
  14.6 5.2 %collective-permute-start.6 = (bf16[256,256]{1,0:T(8,128)(2,1)S(1)}, bf16[256,256]{1,0:T(8,128)(2,1)S(1)}, u32[]{:S(2)}, u32[]{:S(2)}) collective-permute-start(bf16[256,256]{1,0:T(8,128)(2,1)S(1)} %pad_maximum_fusion.14), channel_id=1, source_target_pairs={{0,3},{1,0},{2,1},{3,2},{4,7},{5,4},{6,5},{7,6},{8,11},{9,8},{10,9... | collective-permute-start | bytes 393224 | tf_op jit(solution)/shard_map/ppermute | solution.py:35
  17.3 10.9 %copy-start = (bf16[4,128,7168]{2,1,0:T(8,128)(2,1)S(1)}, bf16[4,128,7168]{2,1,0:T(8,128)(2,1)}, u32[]{:S(2)}) copy-start(bf16[4,128,7168]{2,1,0:T(8,128)(2,1)} %param.7) | copy-start | bytes 22020100
  20.0 14.1 %collective-permute-start.8 = (bf16[64,3712]{1,0:T(8,128)(2,1)S(1)}, bf16[64,3712]{1,0:T(8,128)(2,1)S(1)}, u32[]{:S(2)}, u32[]{:S(2)}) collective-permute-start(bf16[64,3712]{1,0:T(8,128)(2,1)S(1)} %pad_maximum_fusion.1), channel_id=1, source_target_pairs={{0,56},{4,60},{8,0},{12,4},{16,8},{20,12},{24,16},{28,20},{32,24},... | collective-permute-start | bytes 1425416 | tf_op jit(solution)/shard_map/ppermute | solution.py:27
  23.0 12.0 %collective-permute-start.9 = (bf16[64,3712]{1,0:T(8,128)(2,1)S(1)}, bf16[64,3712]{1,0:T(8,128)(2,1)S(1)}, u32[]{:S(2)}, u32[]{:S(2)}) collective-permute-start(bf16[64,3712]{1,0:T(8,128)(2,1)S(1)} %pad_maximum_fusion), channel_id=1, source_target_pairs={{0,8},{4,12},{8,16},{12,20},{16,24},{20,28},{24,32},{28,36},{32,40... | collective-permute-start | bytes 1425416 | tf_op jit(solution)/shard_map/ppermute | solution.py:27
  23.0 8.2 %collective-permute-start.10 = (bf16[48,3712]{1,0:T(8,128)(2,1)S(1)}, bf16[48,3712]{1,0:T(8,128)(2,1)S(1)}, u32[]{:S(2)}, u32[]{:S(2)}) collective-permute-start(bf16[48,3712]{1,0:T(8,128)(2,1)S(1)} %pad_maximum_fusion.7), channel_id=1, source_target_pairs={{0,192},{4,196},{8,200},{12,204},{16,208},{20,212},{24,216},{28,22... | collective-permute-start | bytes 1069064 | tf_op jit(solution)/shard_map/ppermute | solution.py:27
  25.2 8.9 %collective-permute-start.7 = (bf16[48,3712]{1,0:T(8,128)(2,1)S(1)}, bf16[48,3712]{1,0:T(8,128)(2,1)S(1)}, u32[]{:S(2)}, u32[]{:S(2)}) collective-permute-start(bf16[48,3712]{1,0:T(8,128)(2,1)S(1)} %pad_maximum_fusion.6), channel_id=1, source_target_pairs={{0,64},{4,68},{8,72},{12,76},{16,80},{20,84},{24,88},{28,92},{32,9... | collective-permute-start | bytes 1069064 | tf_op jit(solution)/shard_map/ppermute | solution.py:27
  25.2 9.9 %collective-permute-start.11 = (bf16[512,256]{1,0:T(8,128)(2,1)S(1)}, bf16[512,256]{1,0:T(8,128)(2,1)S(1)}, u32[]{:S(2)}, u32[]{:S(2)}) collective-permute-start(bf16[512,256]{1,0:T(8,128)(2,1)S(1)} %pad_maximum_fusion.13.refs_0_), channel_id=1, source_target_pairs={{0,2},{1,3},{2,0},{3,1},{4,6},{5,7},{6,4},{7,5},{8,10},{9,11},{10,... | collective-permute-start | bytes 786440 | tf_op jit(solution)/shard_map/ppermute | solution.py:35
  35.1 10.0 %collective-permute-start.13 = (bf16[64,3712]{1,0:T(8,128)(2,1)S(1)}, bf16[64,3712]{1,0:T(8,128)(2,1)S(1)}, u32[]{:S(2)}, u32[]{:S(2)}) collective-permute-start(bf16[64,3712]{1,0:T(8,128)(2,1)S(1)} %collective-permute-done.8.refs_3_), channel_id=1, source_target_pairs={{0,56},{4,60},{8,0},{12,4},{16,8},{20,12},{24,16},{28,20},{32,24},... | collective-permute-start | bytes 1425416 | tf_op jit(solution)/shard_map/ppermute | solution.py:27
  36.8 8.7 %collective-permute-start.15 = (bf16[64,3712]{1,0:T(8,128)(2,1)S(1)}, bf16[64,3712]{1,0:T(8,128)(2,1)S(1)}, u32[]{:S(2)}, u32[]{:S(2)}) collective-permute-start(bf16[64,3712]{1,0:T(8,128)(2,1)S(1)} %pad_maximum_fusion.3), channel_id=1, source_target_pairs={{0,192},{4,196},{8,200},{12,204},{16,208},{20,212},{24,216},{28,22... | collective-permute-start | bytes 1425416 | tf_op jit(solution)/shard_map/ppermute | solution.py:27
  37.5 9.3 %collective-permute-start.12 = (bf16[64,3712]{1,0:T(8,128)(2,1)S(1)}, bf16[64,3712]{1,0:T(8,128)(2,1)S(1)}, u32[]{:S(2)}, u32[]{:S(2)}) collective-permute-start(bf16[64,3712]{1,0:T(8,128)(2,1)S(1)} %pad_maximum_fusion.2), channel_id=1, source_target_pairs={{0,64},{4,68},{8,72},{12,76},{16,80},{20,84},{24,88},{28,92},{32,9... | collective-permute-start | bytes 1425416 | tf_op jit(solution)/shard_map/ppermute | solution.py:27
  38.3 9.4 %collective-permute-start.14 = (bf16[64,3712]{1,0:T(8,128)(2,1)S(1)}, bf16[64,3712]{1,0:T(8,128)(2,1)S(1)}, u32[]{:S(2)}, u32[]{:S(2)}) collective-permute-start(bf16[64,3712]{1,0:T(8,128)(2,1)S(1)} %collective-permute-done.9.refs_2_), channel_id=1, source_target_pairs={{0,8},{4,12},{8,16},{12,20},{16,24},{20,28},{24,32},{28,36},{32,40... | collective-permute-start | bytes 1425416 | tf_op jit(solution)/shard_map/ppermute | solution.py:27
  38.6 9.9 %collective-permute-start.16 = (bf16[4,128,3584]{2,1,0:T(8,128)(2,1)S(1)}, bf16[4,128,3584]{2,1,0:T(8,128)(2,1)S(1)}, u32[]{:S(2)}, u32[]{:S(2)}) collective-permute-start(bf16[4,128,3584]{2,1,0:T(8,128)(2,1)S(1)} %constant_dynamic-slice_fusion.1), channel_id=1, source_target_pairs={{0,4},{4,0},{8,12},{12,8},{16,20},{20,16},{24,28},{28,24},{32,36},... | collective-permute-start | bytes 11010056 | tf_op jit(solution)/shard_map/ppermute | solution.py:31
  48.5 14.8 %collective-permute-start.18 = (bf16[48,3712]{1,0:T(8,128)(2,1)S(1)}, bf16[48,3712]{1,0:T(8,128)(2,1)S(1)}, u32[]{:S(2)}, u32[]{:S(2)}) collective-permute-start(bf16[48,3712]{1,0:T(8,128)(2,1)S(1)} %slice.170), channel_id=1, source_target_pairs={{0,56},{4,60},{8,0},{12,4},{16,8},{20,12},{24,16},{28,20},{32,24},... | collective-permute-start | bytes 1069064 | tf_op jit(solution)/shard_map/ppermute | solution.py:27
  51.5 12.0 %collective-permute-start.17 = (bf16[64,3712]{1,0:T(8,128)(2,1)S(1)}, bf16[64,3712]{1,0:T(8,128)(2,1)S(1)}, u32[]{:S(2)}, u32[]{:S(2)}) collective-permute-start(bf16[64,3712]{1,0:T(8,128)(2,1)S(1)} %pad_maximum_fusion.4), channel_id=1, source_target_pairs={{0,64},{4,68},{8,72},{12,76},{16,80},{20,84},{24,88},{28,92},{32,9... | collective-permute-start | bytes 1425416 | tf_op jit(solution)/shard_map/ppermute | solution.py:27
  51.5 11.9 %collective-permute-start.20 = (bf16[64,3712]{1,0:T(8,128)(2,1)S(1)}, bf16[64,3712]{1,0:T(8,128)(2,1)S(1)}, u32[]{:S(2)}, u32[]{:S(2)}) collective-permute-start(bf16[64,3712]{1,0:T(8,128)(2,1)S(1)} %pad_maximum_fusion.5), channel_id=1, source_target_pairs={{0,192},{4,196},{8,200},{12,204},{16,208},{20,212},{24,216},{28,22... | collective-permute-start | bytes 1425416 | tf_op jit(solution)/shard_map/ppermute | solution.py:27
  54.1 9.2 %collective-permute-start.19 = (bf16[48,3712]{1,0:T(8,128)(2,1)S(1)}, bf16[48,3712]{1,0:T(8,128)(2,1)S(1)}, u32[]{:S(2)}, u32[]{:S(2)}) collective-permute-start(bf16[48,3712]{1,0:T(8,128)(2,1)S(1)} %pad_maximum_fusion.8), channel_id=1, source_target_pairs={{0,8},{4,12},{8,16},{12,20},{16,24},{20,28},{24,32},{28,36},{32,40... | collective-permute-start | bytes 1069064 | tf_op jit(solution)/shard_map/ppermute | solution.py:27
  58.4 10.6 %copy-start.1 = (s32[64]{0:T(128)S(1)}, s32[64]{0:T(128)}, u32[]{:S(2)}) copy-start(s32[64]{0:T(128)} %constant.51.clone) | copy-start | bytes 772
  58.4 10.6 %copy-start.2 = (s32[64]{0:T(128)S(1)}, s32[64]{0:T(128)}, u32[]{:S(2)}) copy-start(s32[64]{0:T(128)} %constant.52.clone) | copy-start | bytes 772
  58.4 10.6 %copy-start.3 = (s32[64]{0:T(128)S(1)}, s32[64]{0:T(128)}, u32[]{:S(2)}) copy-start(s32[64]{0:T(128)} %constant.53.clone) | copy-start | bytes 772
  63.6 9.7 %collective-permute-start.21 = (bf16[32,3712]{1,0:T(8,128)(2,1)S(1)}, bf16[32,3712]{1,0:T(8,128)(2,1)S(1)}, u32[]{:S(2)}, u32[]{:S(2)}) collective-permute-start(bf16[32,3712]{1,0:T(8,128)(2,1)S(1)} %get-tuple-element.74), channel_id=1, source_target_pairs={{0,64},{4,68},{8,72},{12,76},{16,80},{20,84},{24,88},{28,92},{32,9... | collective-permute-start | bytes 712712 | tf_op jit(solution)/shard_map/ppermute | solution.py:27
  64.4 8.9 %collective-permute-start.22 = (bf16[32,3712]{1,0:T(8,128)(2,1)S(1)}, bf16[32,3712]{1,0:T(8,128)(2,1)S(1)}, u32[]{:S(2)}, u32[]{:S(2)}) collective-permute-start(bf16[32,3712]{1,0:T(8,128)(2,1)S(1)} %get-tuple-element.75), channel_id=1, source_target_pairs={{0,192},{4,196},{8,200},{12,204},{16,208},{20,212},{24,216},{28,22... | collective-permute-start | bytes 712712 | tf_op jit(solution)/shard_map/ppermute | solution.py:27
  66.3 7.0 %collective-permute-start.23 = (bf16[32,3712]{1,0:T(8,128)(2,1)S(1)}, bf16[32,3712]{1,0:T(8,128)(2,1)S(1)}, u32[]{:S(2)}, u32[]{:S(2)}) collective-permute-start(bf16[32,3712]{1,0:T(8,128)(2,1)S(1)} %get-tuple-element.76), channel_id=1, source_target_pairs={{0,8},{4,12},{8,16},{12,20},{16,24},{20,28},{24,32},{28,36},{32,40... | collective-permute-start | bytes 712712 | tf_op jit(solution)/shard_map/ppermute | solution.py:27
  66.3 7.0 %collective-permute-start.24 = (bf16[32,3712]{1,0:T(8,128)(2,1)S(1)}, bf16[32,3712]{1,0:T(8,128)(2,1)S(1)}, u32[]{:S(2)}, u32[]{:S(2)}) collective-permute-start(bf16[32,3712]{1,0:T(8,128)(2,1)S(1)} %get-tuple-element.77), channel_id=1, source_target_pairs={{0,56},{4,60},{8,0},{12,4},{16,8},{20,12},{24,16},{28,20},{32,24},... | collective-permute-start | bytes 712712 | tf_op jit(solution)/shard_map/ppermute | solution.py:27
  69.0 10.8 %collective-permute-start.25 = (bf16[32,3712]{1,0:T(8,128)(2,1)S(1)}, bf16[32,3712]{1,0:T(8,128)(2,1)S(1)}, u32[]{:S(2)}, u32[]{:S(2)}) collective-permute-start(bf16[32,3712]{1,0:T(8,128)(2,1)S(1)} %concatenate.107), channel_id=1, source_target_pairs={{0,72},{4,76},{8,80},{12,84},{16,88},{20,92},{24,96},{28,100},{32,... | collective-permute-start | bytes 712712 | tf_op jit(solution)/shard_map/ppermute | solution.py:27

commit v2 on v1

--- a/solution.py
+++ b/solution.py
@@ -67,30 +67,50 @@
 ]
 
 
-def scores_kernel(places, sizes, where, q_mine, q_other, *refs):
-    slices, pieces = refs[:2], refs[2 : 2 + len(sizes)]
-    out, seq, a_buf, g_buf, w_buf, a_sem, g_sem = refs[2 + len(sizes) :]
+def weights_kernel(names, where, mine, ahead, *refs):
+    outs, rows = refs[:-1], refs[-1]
+    tokens = rows.shape[0] // len(names)
+    for i, ((ox, oz), h) in enumerate(names):
+        u = lax.rem(where[0] + (NX - ox), NX)
+        v = lax.rem(where[1] + (NZ - oz), NZ)
+        at = pl.multiple_of(((u % 2 * NZ + v) * 2 + h) * tokens, tokens)
+        for k, half in enumerate((mine, ahead)):
+
+            @pl.when(u // 2 == k)
+            def _():
+                rows[pl.ds(i * tokens, tokens)] = half[pl.ds(at, tokens)]
+
+    for k, out in enumerate(outs):
+        out[...] = rows[k * WORK : (k + 1) * WORK].astype(jnp.float32).T
+
+
+def turned_weights(where, slices, names, tokens):
+    whole = pl.BlockSpec(memory_space=pltpu.VMEM)
+    count, width = len(names) * tokens, slices[0].shape[1]
+    results = count // WORK
+    return pl.pallas_call(
+        functools.partial(weights_kernel, names),
+        out_shape=[jax.ShapeDtypeStruct((width, WORK), jnp.float32)] * results,
+        in_specs=[pl.BlockSpec(memory_space=pltpu.SMEM), whole, whole],
+        out_specs=[whole] * results,
+        scratch_shapes=[pltpu.VMEM((count, width), jnp.bfloat16)],
+        compiler_params=pltpu.CompilerParams(vmem_limit_bytes=16 << 20),
+        name="weights",
+    )(where, *slices)
+
+
+def scores_kernel(sizes, q_mine, q_other, weights, *refs):
+    pieces = refs[: len(sizes)]
+    out, seq, a_buf, a_sem = refs[len(sizes) :]
     queries, rows, half = q_other.shape
-    tokens = sum(sizes) // len(places)
-    g_copies = [
-        pltpu.make_async_copy(g, g_buf.at[k], g_sem.at[k]) for k, g in enumerate(slices)
-    ]
     count, a_copies = 0, []
     for i, (piece, size) in enumerate(zip(pieces, sizes)):
         a_copies.append(
             pltpu.make_async_copy(piece, a_buf.at[pl.ds(count, size)], a_sem.at[i])
         )
         count += size
-    for copy in g_copies + a_copies:
+    for copy in a_copies:
         copy.start()
-    for copy in g_copies:
-        copy.wait()
-    for i, ((ox, oz), h) in enumerate(places):
-        u = lax.rem(where[0] + (NX - ox), NX)
-        v = lax.rem(where[1] + (NZ - oz), NZ)
-        at = pl.multiple_of(((u % 2 * NZ + v) * 2 + h) * tokens, tokens)
-        w_buf[pl.ds(i * tokens, tokens)] = g_buf[u // 2, pl.ds(at, tokens)]
-    weights = w_buf[...].astype(jnp.float32).T
     for copy in a_copies:
         copy.wait()
     total = [jnp.zeros((1, count), jnp.float32) for _ in range(queries)]
@@ -112,28 +132,23 @@
     seq[...] = jnp.dot(scores, onehot, precision=EXACT, preferred_element_type=jnp.float32)
 
 
-def piece_scores(where, q_mine, q_other, slices, pieces, places):
+def piece_scores(q_mine, q_other, weights, pieces):
     sizes = [piece.shape[0] for piece in pieces]
     count = sum(sizes)
     queries, rows, half = q_other.shape
     anywhere = pl.BlockSpec(memory_space=pl.ANY)
     whole = pl.BlockSpec(memory_space=pltpu.VMEM)
     return pl.pallas_call(
-        functools.partial(scores_kernel, places, sizes),
+        functools.partial(scores_kernel, sizes),
         out_shape=(
             jax.ShapeDtypeStruct((8, count), jnp.float32),
             jax.ShapeDtypeStruct((8, 128), jnp.float32),
         ),
-        in_specs=[pl.BlockSpec(memory_space=pltpu.SMEM)]
-        + [whole] * 2
-        + [anywhere] * (2 + len(pieces)),
+        in_specs=[whole] * 3 + [anywhere] * len(pieces),
         out_specs=[whole, whole],
         scratch_shapes=[
             pltpu.VMEM((count, half + 128), jnp.bfloat16),
-            pltpu.VMEM((2,) + slices[0].shape, jnp.bfloat16),
-            pltpu.VMEM((count, 2 * rows), jnp.bfloat16),
             pltpu.SemaphoreType.DMA((len(pieces),)),
-            pltpu.SemaphoreType.DMA((2,)),
         ],
         compiler_params=pltpu.CompilerParams(vmem_limit_bytes=16 << 20),
         cost_estimate=pl.CostEstimate(
@@ -142,7 +157,7 @@
             transcendentals=0,
         ),
         name="scores",
-    )(where, q_mine, q_other, *slices, *pieces)
+    )(q_mine, q_other, weights, *pieces)
 
 
 def body(query_grads, out_grads, activations, seq_ids):
@@ -172,6 +187,8 @@
     slices = cat([slices, from_col(slices, 1, cols)])
 
     held = {((0, 0), h): own[h * tokens : (h + 1) * tokens] for h in F}
+    order = [((0, 0), h) for h in F]
+    order += [(dst, h) for moves in ROUNDS for _, load in moves for _, part, dst in load for h in part]
     slots, scores, by_seq = [], [], []
     waiting = [(own, [((0, 0), h) for h in F])]
 
@@ -182,7 +199,7 @@
             pieces.append(piece)
             places.extend(names)
             count += piece.shape[0]
-        part, seq = piece_scores(where, q_mine, q_other, slices, pieces, places)
+        part, seq = piece_scores(q_mine, q_other, weights[len(scores)], pieces)
         scores.append(part)
         by_seq.append(seq)
         slots.extend(places)
@@ -199,8 +216,9 @@
                 (sent, slices, q_slice, q_mine)
             )
             q_other = swap(q_slice)
+            weights = turned_weights(where, slices, order, tokens)
         if number == 3:
-            sent, slices, q_other = lax.optimization_barrier((sent, slices, q_other))
+            sent, weights, q_other = lax.optimization_barrier((sent, weights, q_other))
             work()
             work()
         if number == 4:

time: 115 us -> 114 us (level)
    pallas_call x4 -> x5, Pallas kernels: 18.3 us -> 17.4 us  [the longest x4 15.2 us: piece_scores(): pl.pallas_call(functools.partial(scores_kernel, sizes), out_shape=(jax.Sh...]
  transfers between devices with their start and end apart: 26 -> 26, of which waited for: 10 -> 13; matrix products, arithmetic and copies ran while one was open for 4% -> 4% of each run, Pallas kernels for 12% -> 12%
where the time goes in v2:
time: 114 us
  starting transfers between devices  39.2 us (34%)
  blocking collectives  27.3 us (24%)
  waiting for transfers between devices  20 us (18%)
  Pallas kernels  17.4 us (15%)
  local copies, waits for them, and re-layouts  6.17 us (5%)
  other arithmetic  2.44 us (2%)
    all_to_all x1, blocking collectives, body(): arrived = lax.all_to_all(parts, ('row', 'col'), 0, 0, tiled=True)  27.3 us
    ppermute x21, starting transfers between devices, shift(): return lax.ppermute(block, 'row', pairs)  26.3 us
    ppermute x21, waiting for transfers between devices, shift(): return lax.ppermute(block, 'row', pairs)  18.1 us
    pallas_call x4, Pallas kernels, piece_scores(): pl.pallas_call(functools.partial(scores_kernel, sizes), out_shape=(jax.Sh...  15.2 us
    ppermute x3, starting transfers between devices, swap(): return lax.ppermute(block, 'row', [(i, i ^ 1) for i in range(NX * NZ * 2)])  7.27 us
    ppermute x2, starting transfers between devices, from_col(): lax.ppermute(block, 'col', [(i, (i - ahead) % cols) for i in range(cols)])  5.65 us
    dynamic_slice x3, local copies, waits for them, and re-layouts, columns(): return lax.dynamic_slice(array, start, array.shape[:-1] + (half,))  3.63 us
  transfers between devices with their start and end apart: 26, of which 13 were waited for; matrix products, arithmetic and copies ran while one was open for 4% of the time, Pallas kernels for 12%

profile of v2, /device:TPU:1, one launch (start us, length us, event | category | flops | bytes accessed | tf_op | source)
XLA Modules:
  0.0 113.9 jit_solution(1785993861706292017)
XLA Ops:
  0.6 0.7 convert_element_type.5
  1.3 1.0 constant_dynamic-slice_fusion.3
  2.4 3.3 %collective-permute-start = (bf16[16,3712]{1,0:T(8,128)(2,1)S(1)}, bf16[16,3712]{1,0:T(8,128)(2,1)S(1)}, u32[]{:S(2)}, u32[]{:S(2)}) collective-permute-start(bf16[16,3712]{1,0:T(8,128)(2,1)S(1)} %pad_maximum_fusion.15), channel_id=1, source_target_pairs={{0,4},{4,0},{8,12},{12,8},{16,20},{20,16},{24,28},{28,24},{32,36},... | collective-permute-start | bytes 356360 | tf_op jit(solution)/shard_map/ppermute | solution.py:31
  5.7 0.1 collective-permute-start.5
  5.9 1.3 %collective-permute-done.5 = bf16[256,128]{1,0:T(8,128)(2,1)S(1)} collective-permute-done((bf16[256,128]{1,0:T(8,128)(2,1)}, bf16[256,128]{1,0:T(8,128)(2,1)S(1)}, u32[]{:S(2)}, u32[]{:S(2)}) %collective-permute-start.5) | collective-permute-done | bytes 65568 | tf_op jit(solution)/shard_map/ppermute | solution.py:31
  7.2 0.9 pad_maximum_fusion.14
  8.2 2.4 %collective-permute-start.3 = (bf16[32,3712]{1,0:T(8,128)(2,1)S(1)}, bf16[32,3712]{1,0:T(8,128)(2,1)S(1)}, u32[]{:S(2)}, u32[]{:S(2)}) collective-permute-start(bf16[32,3712]{1,0:T(8,128)(2,1)S(1)} %maximum_select_fusion.refs_0_), channel_id=1, source_target_pairs={{0,192},{4,196},{8,200},{12,204},{16,208},{20,212},{24,216},{28,22... | collective-permute-start | bytes 712712 | tf_op jit(solution)/shard_map/ppermute | solution.py:27
  10.5 4.0 %collective-permute-start.4 = (bf16[32,3712]{1,0:T(8,128)(2,1)S(1)}, bf16[32,3712]{1,0:T(8,128)(2,1)S(1)}, u32[]{:S(2)}, u32[]{:S(2)}) collective-permute-start(bf16[32,3712]{1,0:T(8,128)(2,1)S(1)} %maximum_select_fusion.refs_0_), channel_id=1, source_target_pairs={{0,56},{4,60},{8,0},{12,4},{16,8},{20,12},{24,16},{28,20},{32,24},... | collective-permute-start | bytes 712712 | tf_op jit(solution)/shard_map/ppermute | solution.py:27
  14.6 2.7 %collective-permute-start.6 = (bf16[256,256]{1,0:T(8,128)(2,1)S(1)}, bf16[256,256]{1,0:T(8,128)(2,1)S(1)}, u32[]{:S(2)}, u32[]{:S(2)}) collective-permute-start(bf16[256,256]{1,0:T(8,128)(2,1)S(1)} %pad_maximum_fusion.14), channel_id=1, source_target_pairs={{0,3},{1,0},{2,1},{3,2},{4,7},{5,4},{6,5},{7,6},{8,11},{9,8},{10,9... | collective-permute-start | bytes 393224 | tf_op jit(solution)/shard_map/ppermute | solution.py:35
  17.3 2.4 %constant_dynamic-slice_fusion.1 = bf16[4,128,3584]{2,1,0:T(8,128)(2,1)S(1)} fusion(bf16[4,128,7168]{2,1,0:T(8,128)(2,1)} %param.7, s32[]{:T(128)S(6)} %select_n.18), kind=kLoop, calls=%fused_computation.31 | loop fusion | bytes 7340036 | tf_op jit(solution)/shard_map/dynamic_slice | solution.py:175
  20.0 2.9 %collective-permute-start.8 = (bf16[64,3712]{1,0:T(8,128)(2,1)S(1)}, bf16[64,3712]{1,0:T(8,128)(2,1)S(1)}, u32[]{:S(2)}, u32[]{:S(2)}) collective-permute-start(bf16[64,3712]{1,0:T(8,128)(2,1)S(1)} %pad_maximum_fusion.1), channel_id=1, source_target_pairs={{0,56},{4,60},{8,0},{12,4},{16,8},{20,12},{24,16},{28,20},{32,24},... | collective-permute-start | bytes 1425416 | tf_op jit(solution)/shard_map/ppermute | solution.py:27
  23.0 2.3 %collective-permute-start.10 = (bf16[48,3712]{1,0:T(8,128)(2,1)S(1)}, bf16[48,3712]{1,0:T(8,128)(2,1)S(1)}, u32[]{:S(2)}, u32[]{:S(2)}) collective-permute-start(bf16[48,3712]{1,0:T(8,128)(2,1)S(1)} %pad_maximum_fusion.7), channel_id=1, source_target_pairs={{0,192},{4,196},{8,200},{12,204},{16,208},{20,212},{24,216},{28,22... | collective-permute-start | bytes 1069064 | tf_op jit(solution)/shard_map/ppermute | solution.py:27
  25.2 2.9 %collective-permute-start.11 = (bf16[512,256]{1,0:T(8,128)(2,1)S(1)}, bf16[512,256]{1,0:T(8,128)(2,1)S(1)}, u32[]{:S(2)}, u32[]{:S(2)}) collective-permute-start(bf16[512,256]{1,0:T(8,128)(2,1)S(1)} %pad_maximum_fusion.13.mine), channel_id=1, source_target_pairs={{0,2},{1,3},{2,0},{3,1},{4,6},{5,7},{6,4},{7,5},{8,10},{9,11},{10,... | collective-permute-start | bytes 786440 | tf_op jit(solution)/shard_map/ppermute | solution.py:35
  28.2 0.2 constant_dynamic-slice_fusion.q_mine
  28.4 2.8 %collective-permute-done.10.refs_6_ = bf16[48,3712]{1,0:T(8,128)(2,1)S(1)} collective-permute-done((bf16[48,3712]{1,0:T(8,128)(2,1)S(1)}, bf16[48,3712]{1,0:T(8,128)(2,1)S(1)}, u32[]{:S(2)}, u32[]{:S(2)}) %collective-permute-start.10) | collective-permute-done | bytes 356384 | tf_op jit(solution)/shard_map/ppermute | solution.py:27
  31.2 2.9 %collective-permute-done.7.refs_5_ = bf16[48,3712]{1,0:T(8,128)(2,1)S(1)} collective-permute-done((bf16[48,3712]{1,0:T(8,128)(2,1)S(1)}, bf16[48,3712]{1,0:T(8,128)(2,1)S(1)}, u32[]{:S(2)}, u32[]{:S(2)}) %collective-permute-start.7) | collective-permute-done | bytes 356384 | tf_op jit(solution)/shard_map/ppermute | solution.py:27
  34.1 0.8 collective-permute-done.9.refs_0_
  35.1 1.7 %collective-permute-start.13 = (bf16[64,3712]{1,0:T(8,128)(2,1)S(1)}, bf16[64,3712]{1,0:T(8,128)(2,1)S(1)}, u32[]{:S(2)}, u32[]{:S(2)}) collective-permute-start(bf16[64,3712]{1,0:T(8,128)(2,1)S(1)} %collective-permute-done.8.refs_1_), channel_id=1, source_target_pairs={{0,56},{4,60},{8,0},{12,4},{16,8},{20,12},{24,16},{28,20},{32,24},... | collective-permute-start | bytes 1425416 | tf_op jit(solution)/shard_map/ppermute | solution.py:27
  36.8 0.7 collective-permute-start.15
  37.5 0.8 collective-permute-start.12
  38.3 0.4 collective-permute-start.14
  38.6 3.8 %collective-permute-start.16 = (bf16[4,128,3584]{2,1,0:T(8,128)(2,1)S(1)}, bf16[4,128,3584]{2,1,0:T(8,128)(2,1)S(1)}, u32[]{:S(2)}, u32[]{:S(2)}) collective-permute-start(bf16[4,128,3584]{2,1,0:T(8,128)(2,1)S(1)} %constant_dynamic-slice_fusion.1), channel_id=1, source_target_pairs={{0,4},{4,0},{8,12},{12,8},{16,20},{20,16},{24,28},{28,24},{32,36},... | collective-permute-start | bytes 11010056 | tf_op jit(solution)/shard_map/ppermute | solution.py:31
  42.5 2.2 %weights.1 = (f32[256,256]{1,0:T(8,128)S(1)}, f32[256,256]{1,0:T(8,128)S(1)}, f32[256,256]{1,0:T(8,128)S(1)}, f32[256,256]{1,0:T(8,128)S(1)}) custom-call(s32[2]{0:T(128)S(1)} %pad_add_fusion.where, bf16[512,256]{1,0:T(8,128)(2,1)S(1)} %pad_maximum_fusion.13.mine, bf16[512,256]{1,0:T(8,128)(2,1)S(1)} %collective-permute-done.11.ahead), custom_call_target="tpu_custom_call" | custom-call | tf_op jit(solution)/shard_map/weights/pallas_call | solution.py:91
  44.6 0.4 collective-permute-done.13.refs_1_
  45.1 0.4 collective-permute-done.15.refs_3_
  45.5 1.2 %collective-permute-done.12.refs_2_ = bf16[64,3712]{1,0:T(8,128)(2,1)S(1)} collective-permute-done((bf16[64,3712]{1,0:T(8,128)(2,1)S(1)}, bf16[64,3712]{1,0:T(8,128)(2,1)S(1)}, u32[]{:S(2)}, u32[]{:S(2)}) %collective-permute-start.12) | collective-permute-done | bytes 475168 | tf_op jit(solution)/shard_map/ppermute | solution.py:27
  46.8 0.9 collective-permute-done.14.refs_0_
  47.8 0.7 collective-permute-done.16.q_other
  48.5 3.0 %collective-permute-start.18 = (bf16[48,3712]{1,0:T(8,128)(2,1)S(1)}, bf16[48,3712]{1,0:T(8,128)(2,1)S(1)}, u32[]{:S(2)}, u32[]{:S(2)}) collective-permute-start(bf16[48,3712]{1,0:T(8,128)(2,1)S(1)} %slice.170), channel_id=1, source_target_pairs={{0,56},{4,60},{8,0},{12,4},{16,8},{20,12},{24,16},{28,20},{32,24},... | collective-permute-start | bytes 1069064 | tf_op jit(solution)/shard_map/ppermute | solution.py:27
  51.5 2.7 %collective-permute-start.20 = (bf16[64,3712]{1,0:T(8,128)(2,1)S(1)}, bf16[64,3712]{1,0:T(8,128)(2,1)S(1)}, u32[]{:S(2)}, u32[]{:S(2)}) collective-permute-start(bf16[64,3712]{1,0:T(8,128)(2,1)S(1)} %pad_maximum_fusion.5), channel_id=1, source_target_pairs={{0,192},{4,196},{8,200},{12,204},{16,208},{20,212},{24,216},{28,22... | collective-permute-start | bytes 1425416 | tf_op jit(solution)/shard_map/ppermute | solution.py:27
  54.1 3.5 %scores.5 = (f32[8,256]{1,0:T(8,128)S(1)}, f32[8,128]{1,0:T(8,128)S(1)}) custom-call(bf16[4,128,3584]{2,1,0:T(8,128)(2,1)S(1)} %constant_dynamic-slice_fusion.q_mine, bf16[4,128,3584]{2,1,0:T(8,128)(2,1)S(1)} %collective-permute-done.16.q_other, f32[256,256]{1,0:T(8,128)S(1)} %get-tuple-element.79.weights, ...), custom_call_target="tpu_custom_call" | custom-call | flops 1879048192 | bytes 9175040 | tf_op jit(solution)/shard_map/scores/pallas_call | solution.py:141
  57.6 4.1 %scores.4 = (f32[8,256]{1,0:T(8,128)S(1)}, f32[8,128]{1,0:T(8,128)S(1)}) custom-call(bf16[4,128,3584]{2,1,0:T(8,128)(2,1)S(1)} %constant_dynamic-slice_fusion.q_mine, bf16[4,128,3584]{2,1,0:T(8,128)(2,1)S(1)} %collective-permute-done.16.q_other, f32[256,256]{1,0:T(8,128)S(1)} %get-tuple-element.77.weights, bf16[32,3712]{1,0:T(8,128)(2,1)S(1)} %maximum_select_fusion.refs_0_, ...), custom_call_target="tpu_custom_call" | custom-call | flops 1879048192 | bytes 9175040 | tf_op jit(solution)/shard_map/scores/pallas_call | solution.py:141
  61.8 1.1 collective-permute-done.19.refs_0_
  63.0 0.3 collective-permute-done.17.refs_2_
  63.4 0.9 collective-permute-start.21
  64.4 1.8 %collective-permute-start.22 = (bf16[32,3712]{1,0:T(8,128)(2,1)S(1)}, bf16[32,3712]{1,0:T(8,128)(2,1)S(1)}, u32[]{:S(2)}, u32[]{:S(2)}) collective-permute-start(bf16[32,3712]{1,0:T(8,128)(2,1)S(1)} %get-tuple-element.87), channel_id=1, source_target_pairs={{0,192},{4,196},{8,200},{12,204},{16,208},{20,212},{24,216},{28,22... | collective-permute-start | bytes 712712 | tf_op jit(solution)/shard_map/ppermute | solution.py:27
  66.2 2.7 %collective-permute-start.24 = (bf16[32,3712]{1,0:T(8,128)(2,1)S(1)}, bf16[32,3712]{1,0:T(8,128)(2,1)S(1)}, u32[]{:S(2)}, u32[]{:S(2)}) collective-permute-start(bf16[32,3712]{1,0:T(8,128)(2,1)S(1)} %get-tuple-element.89), channel_id=1, source_target_pairs={{0,56},{4,60},{8,0},{12,4},{16,8},{20,12},{24,16},{28,20},{32,24},... | collective-permute-start | bytes 712712 | tf_op jit(solution)/shard_map/ppermute | solution.py:27
  68.9 3.5 %scores.6 = (f32[8,256]{1,0:T(8,128)S(1)}, f32[8,128]{1,0:T(8,128)S(1)}) custom-call(bf16[4,128,3584]{2,1,0:T(8,128)(2,1)S(1)} %constant_dynamic-slice_fusion.q_mine, bf16[4,128,3584]{2,1,0:T(8,128)(2,1)S(1)} %collective-permute-done.16.q_other, f32[256,256]{1,0:T(8,128)S(1)} %get-tuple-element.83.weights, ...), custom_call_target="tpu_custom_call" | custom-call | flops 1879048192 | bytes 9175040 | tf_op jit(solution)/shard_map/scores/pallas_call | solution.py:141
  72.4 0.2 collective-permute-done.23.refs_4_
  72.7 7.0 %collective-permute-done.25.refs_6_ = bf16[32,3712]{1,0:T(8,128)(2,1)S(1)} collective-permute-done((bf16[32,3712]{1,0:T(8,128)(2,1)S(1)}, bf16[32,3712]{1,0:T(8,128)(2,1)S(1)}, u32[]{:S(2)}, u32[]{:S(2)}) %collective-permute-start.25) | collective-permute-done | bytes 237600 | tf_op jit(solution)/shard_map/ppermute | solution.py:27
  79.6 4.1 %scores.7 = (f32[8,256]{1,0:T(8,128)S(1)}, f32[8,128]{1,0:T(8,128)S(1)}) custom-call(bf16[4,128,3584]{2,1,0:T(8,128)(2,1)S(1)} %constant_dynamic-slice_fusion.q_mine, bf16[4,128,3584]{2,1,0:T(8,128)(2,1)S(1)} %collective-permute-done.16.q_other, f32[256,256]{1,0:T(8,128)S(1)} %get-tuple-element.85.weights, ...), custom_call_target="tpu_custom_call" | custom-call | flops 1879048192 | bytes 9175040 | tf_op jit(solution)/shard_map/scores/pallas_call | solution.py:141
  83.9 0.1 reshape.40
  84.1 0.3 fusion.1
  84.5 0.4 all_to_all.8
  84.9 27.3 %all_to_all.10 = f32[256,1,192]{2,1,0:T(1,128)S(1)} all-to-all(f32[256,1,192]{2,1,0:T(1,128)S(1)} %all_to_all.8), channel_id=1, replica_groups=mesh['row'=64,'col'=4] {'row','col'}, dimensions={0} | all-to-all | bytes 393216 | tf_op jit(solution)/shard_map/all_to_all | solution.py:252
  112.2 0.3 reduce_sum.9
  112.6 0.7 reshape.41
  113.2 0.7 reshape.42
  (76 shorter events, 1.5 us)
Async XLA Ops:
  2.4 5.7 %collective-permute-start = (bf16[16,3712]{1,0:T(8,128)(2,1)S(1)}, bf16[16,3712]{1,0:T(8,128)(2,1)S(1)}, u32[]{:S(2)}, u32[]{:S(2)}) collective-permute-start(bf16[16,3712]{1,0:T(8,128)(2,1)S(1)} %pad_maximum_fusion.15), channel_id=1, source_target_pairs={{0,4},{4,0},{8,12},{12,8},{16,20},{20,16},{24,28},{28,24},{32,36},... | collective-permute-start | bytes 356360 | tf_op jit(solution)/shard_map/ppermute | solution.py:31
  5.7 1.5 %collective-permute-start.5 = (bf16[256,128]{1,0:T(8,128)(2,1)}, bf16[256,128]{1,0:T(8,128)(2,1)S(1)}, u32[]{:S(2)}, u32[]{:S(2)}) collective-permute-start(bf16[256,128]{1,0:T(8,128)(2,1)} %param.8), channel_id=1, source_target_pairs={{0,4},{4,0},{8,12},{12,8},{16,20},{20,16},{24,28},{28,24},{32,36},... | collective-permute-start | bytes 196616 | tf_op jit(solution)/shard_map/ppermute | solution.py:31
  8.1 11.8 %collective-permute-start.2 = (bf16[32,3712]{1,0:T(8,128)(2,1)S(1)}, bf16[32,3712]{1,0:T(8,128)(2,1)S(1)}, u32[]{:S(2)}, u32[]{:S(2)}) collective-permute-start(bf16[32,3712]{1,0:T(8,128)(2,1)S(1)} %maximum_select_fusion.refs_0_), channel_id=1, source_target_pairs={{0,8},{4,12},{8,16},{12,20},{16,24},{20,28},{24,32},{28,36},{32,40... | collective-permute-start | bytes 712712 | tf_op jit(solution)/shard_map/ppermute | solution.py:27
  8.2 11.6 %collective-permute-start.3 = (bf16[32,3712]{1,0:T(8,128)(2,1)S(1)}, bf16[32,3712]{1,0:T(8,128)(2,1)S(1)}, u32[]{:S(2)}, u32[]{:S(2)}) collective-permute-start(bf16[32,3712]{1,0:T(8,128)(2,1)S(1)} %maximum_select_fusion.refs_0_), channel_id=1, source_target_pairs={{0,192},{4,196},{8,200},{12,204},{16,208},{20,212},{24,216},{28,22... | collective-permute-start | bytes 712712 | tf_op jit(solution)/shard_map/ppermute | solution.py:27
  10.5 9.3 %collective-permute-start.1 = (bf16[32,3712]{1,0:T(8,128)(2,1)S(1)}, bf16[32,3712]{1,0:T(8,128)(2,1)S(1)}, u32[]{:S(2)}, u32[]{:S(2)}) collective-permute-start(bf16[32,3712]{1,0:T(8,128)(2,1)S(1)} %maximum_select_fusion.refs_0_), channel_id=1, source_target_pairs={{0,64},{4,68},{8,72},{12,76},{16,80},{20,84},{24,88},{28,92},{32,9... | collective-permute-start | bytes 712712 | tf_op jit(solution)/shard_map/ppermute | solution.py:27
  10.5 9.3 %collective-permute-start.4 = (bf16[32,3712]{1,0:T(8,128)(2,1)S(1)}, bf16[32,3712]{1,0:T(8,128)(2,1)S(1)}, u32[]{:S(2)}, u32[]{:S(2)}) collective-permute-start(bf16[32,3712]{1,0:T(8,128)(2,1)S(1)} %maximum_select_fusion.refs_0_), channel_id=1, source_target_pairs={{0,56},{4,60},{8,0},{12,4},{16,8},{20,12},{24,16},{28,20},{32,24},... | collective-permute-start | bytes 712712 | tf_op jit(solution)/shard_map/ppermute | solution.py:27
  14.6 5.2 %collective-permute-start.6 = (bf16[256,256]{1,0:T(8,128)(2,1)S(1)}, bf16[256,256]{1,0:T(8,128)(2,1)S(1)}, u32[]{:S(2)}, u32[]{:S(2)}) collective-permute-start(bf16[256,256]{1,0:T(8,128)(2,1)S(1)} %pad_maximum_fusion.14), channel_id=1, source_target_pairs={{0,3},{1,0},{2,1},{3,2},{4,7},{5,4},{6,5},{7,6},{8,11},{9,8},{10,9... | collective-permute-start | bytes 393224 | tf_op jit(solution)/shard_map/ppermute | solution.py:35
  17.3 10.9 %copy-start = (bf16[4,128,7168]{2,1,0:T(8,128)(2,1)S(1)}, bf16[4,128,7168]{2,1,0:T(8,128)(2,1)}, u32[]{:S(2)}) copy-start(bf16[4,128,7168]{2,1,0:T(8,128)(2,1)} %param.7) | copy-start | bytes 22020100
  20.0 14.1 %collective-permute-start.8 = (bf16[64,3712]{1,0:T(8,128)(2,1)S(1)}, bf16[64,3712]{1,0:T(8,128)(2,1)S(1)}, u32[]{:S(2)}, u32[]{:S(2)}) collective-permute-start(bf16[64,3712]{1,0:T(8,128)(2,1)S(1)} %pad_maximum_fusion.1), channel_id=1, source_target_pairs={{0,56},{4,60},{8,0},{12,4},{16,8},{20,12},{24,16},{28,20},{32,24},... | collective-permute-start | bytes 1425416 | tf_op jit(solution)/shard_map/ppermute | solution.py:27
  22.9 12.0 %collective-permute-start.9 = (bf16[64,3712]{1,0:T(8,128)(2,1)S(1)}, bf16[64,3712]{1,0:T(8,128)(2,1)S(1)}, u32[]{:S(2)}, u32[]{:S(2)}) collective-permute-start(bf16[64,3712]{1,0:T(8,128)(2,1)S(1)} %pad_maximum_fusion), channel_id=1, source_target_pairs={{0,8},{4,12},{8,16},{12,20},{16,24},{20,28},{24,32},{28,36},{32,40... | collective-permute-start | bytes 1425416 | tf_op jit(solution)/shard_map/ppermute | solution.py:27
  23.0 8.2 %collective-permute-start.10 = (bf16[48,3712]{1,0:T(8,128)(2,1)S(1)}, bf16[48,3712]{1,0:T(8,128)(2,1)S(1)}, u32[]{:S(2)}, u32[]{:S(2)}) collective-permute-start(bf16[48,3712]{1,0:T(8,128)(2,1)S(1)} %pad_maximum_fusion.7), channel_id=1, source_target_pairs={{0,192},{4,196},{8,200},{12,204},{16,208},{20,212},{24,216},{28,22... | collective-permute-start | bytes 1069064 | tf_op jit(solution)/shard_map/ppermute | solution.py:27
  25.2 8.9 %collective-permute-start.7 = (bf16[48,3712]{1,0:T(8,128)(2,1)S(1)}, bf16[48,3712]{1,0:T(8,128)(2,1)S(1)}, u32[]{:S(2)}, u32[]{:S(2)}) collective-permute-start(bf16[48,3712]{1,0:T(8,128)(2,1)S(1)} %pad_maximum_fusion.6), channel_id=1, source_target_pairs={{0,64},{4,68},{8,72},{12,76},{16,80},{20,84},{24,88},{28,92},{32,9... | collective-permute-start | bytes 1069064 | tf_op jit(solution)/shard_map/ppermute | solution.py:27
  25.2 9.9 %collective-permute-start.11 = (bf16[512,256]{1,0:T(8,128)(2,1)S(1)}, bf16[512,256]{1,0:T(8,128)(2,1)S(1)}, u32[]{:S(2)}, u32[]{:S(2)}) collective-permute-start(bf16[512,256]{1,0:T(8,128)(2,1)S(1)} %pad_maximum_fusion.13.mine), channel_id=1, source_target_pairs={{0,2},{1,3},{2,0},{3,1},{4,6},{5,7},{6,4},{7,5},{8,10},{9,11},{10,... | collective-permute-start | bytes 786440 | tf_op jit(solution)/shard_map/ppermute | solution.py:35
  35.1 10.0 %collective-permute-start.13 = (bf16[64,3712]{1,0:T(8,128)(2,1)S(1)}, bf16[64,3712]{1,0:T(8,128)(2,1)S(1)}, u32[]{:S(2)}, u32[]{:S(2)}) collective-permute-start(bf16[64,3712]{1,0:T(8,128)(2,1)S(1)} %collective-permute-done.8.refs_1_), channel_id=1, source_target_pairs={{0,56},{4,60},{8,0},{12,4},{16,8},{20,12},{24,16},{28,20},{32,24},... | collective-permute-start | bytes 1425416 | tf_op jit(solution)/shard_map/ppermute | solution.py:27
  36.8 8.7 %collective-permute-start.15 = (bf16[64,3712]{1,0:T(8,128)(2,1)S(1)}, bf16[64,3712]{1,0:T(8,128)(2,1)S(1)}, u32[]{:S(2)}, u32[]{:S(2)}) collective-permute-start(bf16[64,3712]{1,0:T(8,128)(2,1)S(1)} %pad_maximum_fusion.3), channel_id=1, source_target_pairs={{0,192},{4,196},{8,200},{12,204},{16,208},{20,212},{24,216},{28,22... | collective-permute-start | bytes 1425416 | tf_op jit(solution)/shard_map/ppermute | solution.py:27
  37.5 9.3 %collective-permute-start.12 = (bf16[64,3712]{1,0:T(8,128)(2,1)S(1)}, bf16[64,3712]{1,0:T(8,128)(2,1)S(1)}, u32[]{:S(2)}, u32[]{:S(2)}) collective-permute-start(bf16[64,3712]{1,0:T(8,128)(2,1)S(1)} %pad_maximum_fusion.2), channel_id=1, source_target_pairs={{0,64},{4,68},{8,72},{12,76},{16,80},{20,84},{24,88},{28,92},{32,9... | collective-permute-start | bytes 1425416 | tf_op jit(solution)/shard_map/ppermute | solution.py:27
  38.3 9.4 %collective-permute-start.14 = (bf16[64,3712]{1,0:T(8,128)(2,1)S(1)}, bf16[64,3712]{1,0:T(8,128)(2,1)S(1)}, u32[]{:S(2)}, u32[]{:S(2)}) collective-permute-start(bf16[64,3712]{1,0:T(8,128)(2,1)S(1)} %collective-permute-done.9.refs_0_), channel_id=1, source_target_pairs={{0,8},{4,12},{8,16},{12,20},{16,24},{20,28},{24,32},{28,36},{32,40... | collective-permute-start | bytes 1425416 | tf_op jit(solution)/shard_map/ppermute | solution.py:27
  38.6 9.9 %collective-permute-start.16 = (bf16[4,128,3584]{2,1,0:T(8,128)(2,1)S(1)}, bf16[4,128,3584]{2,1,0:T(8,128)(2,1)S(1)}, u32[]{:S(2)}, u32[]{:S(2)}) collective-permute-start(bf16[4,128,3584]{2,1,0:T(8,128)(2,1)S(1)} %constant_dynamic-slice_fusion.1), channel_id=1, source_target_pairs={{0,4},{4,0},{8,12},{12,8},{16,20},{20,16},{24,28},{28,24},{32,36},... | collective-permute-start | bytes 11010056 | tf_op jit(solution)/shard_map/ppermute | solution.py:31
  48.5 13.3 %collective-permute-start.18 = (bf16[48,3712]{1,0:T(8,128)(2,1)S(1)}, bf16[48,3712]{1,0:T(8,128)(2,1)S(1)}, u32[]{:S(2)}, u32[]{:S(2)}) collective-permute-start(bf16[48,3712]{1,0:T(8,128)(2,1)S(1)} %slice.170), channel_id=1, source_target_pairs={{0,56},{4,60},{8,0},{12,4},{16,8},{20,12},{24,16},{28,20},{32,24},... | collective-permute-start | bytes 1069064 | tf_op jit(solution)/shard_map/ppermute | solution.py:27
  51.5 11.9 %collective-permute-start.17 = (bf16[64,3712]{1,0:T(8,128)(2,1)S(1)}, bf16[64,3712]{1,0:T(8,128)(2,1)S(1)}, u32[]{:S(2)}, u32[]{:S(2)}) collective-permute-start(bf16[64,3712]{1,0:T(8,128)(2,1)S(1)} %pad_maximum_fusion.4), channel_id=1, source_target_pairs={{0,64},{4,68},{8,72},{12,76},{16,80},{20,84},{24,88},{28,92},{32,9... | collective-permute-start | bytes 1425416 | tf_op jit(solution)/shard_map/ppermute | solution.py:27
  51.5 11.5 %collective-permute-start.20 = (bf16[64,3712]{1,0:T(8,128)(2,1)S(1)}, bf16[64,3712]{1,0:T(8,128)(2,1)S(1)}, u32[]{:S(2)}, u32[]{:S(2)}) collective-permute-start(bf16[64,3712]{1,0:T(8,128)(2,1)S(1)} %pad_maximum_fusion.5), channel_id=1, source_target_pairs={{0,192},{4,196},{8,200},{12,204},{16,208},{20,212},{24,216},{28,22... | collective-permute-start | bytes 1425416 | tf_op jit(solution)/shard_map/ppermute | solution.py:27
  54.1 8.8 %collective-permute-start.19 = (bf16[48,3712]{1,0:T(8,128)(2,1)S(1)}, bf16[48,3712]{1,0:T(8,128)(2,1)S(1)}, u32[]{:S(2)}, u32[]{:S(2)}) collective-permute-start(bf16[48,3712]{1,0:T(8,128)(2,1)S(1)} %pad_maximum_fusion.8), channel_id=1, source_target_pairs={{0,8},{4,12},{8,16},{12,20},{16,24},{20,28},{24,32},{28,36},{32,40... | collective-permute-start | bytes 1069064 | tf_op jit(solution)/shard_map/ppermute | solution.py:27
  57.6 11.3 %copy-start.1 = (s32[64]{0:T(128)S(1)}, s32[64]{0:T(128)}, u32[]{:S(2)}) copy-start(s32[64]{0:T(128)} %constant.51.clone) | copy-start | bytes 772
  57.6 11.3 %copy-start.2 = (s32[64]{0:T(128)S(1)}, s32[64]{0:T(128)}, u32[]{:S(2)}) copy-start(s32[64]{0:T(128)} %constant.52.clone) | copy-start | bytes 772
  57.6 11.3 %copy-start.3 = (s32[64]{0:T(128)S(1)}, s32[64]{0:T(128)}, u32[]{:S(2)}) copy-start(s32[64]{0:T(128)} %constant.53.clone) | copy-start | bytes 772
  63.4 9.0 %collective-permute-start.21 = (bf16[32,3712]{1,0:T(8,128)(2,1)S(1)}, bf16[32,3712]{1,0:T(8,128)(2,1)S(1)}, u32[]{:S(2)}, u32[]{:S(2)}) collective-permute-start(bf16[32,3712]{1,0:T(8,128)(2,1)S(1)} %get-tuple-element.86), channel_id=1, source_target_pairs={{0,64},{4,68},{8,72},{12,76},{16,80},{20,84},{24,88},{28,92},{32,9... | collective-permute-start | bytes 712712 | tf_op jit(solution)/shard_map/ppermute | solution.py:27
  64.4 8.0 %collective-permute-start.22 = (bf16[32,3712]{1,0:T(8,128)(2,1)S(1)}, bf16[32,3712]{1,0:T(8,128)(2,1)S(1)}, u32[]{:S(2)}, u32[]{:S(2)}) collective-permute-start(bf16[32,3712]{1,0:T(8,128)(2,1)S(1)} %get-tuple-element.87), channel_id=1, source_target_pairs={{0,192},{4,196},{8,200},{12,204},{16,208},{20,212},{24,216},{28,22... | collective-permute-start | bytes 712712 | tf_op jit(solution)/shard_map/ppermute | solution.py:27
  66.2 6.5 %collective-permute-start.23 = (bf16[32,3712]{1,0:T(8,128)(2,1)S(1)}, bf16[32,3712]{1,0:T(8,128)(2,1)S(1)}, u32[]{:S(2)}, u32[]{:S(2)}) collective-permute-start(bf16[32,3712]{1,0:T(8,128)(2,1)S(1)} %get-tuple-element.88), channel_id=1, source_target_pairs={{0,8},{4,12},{8,16},{12,20},{16,24},{20,28},{24,32},{28,36},{32,40... | collective-permute-start | bytes 712712 | tf_op jit(solution)/shard_map/ppermute | solution.py:27
  66.2 6.5 %collective-permute-start.24 = (bf16[32,3712]{1,0:T(8,128)(2,1)S(1)}, bf16[32,3712]{1,0:T(8,128)(2,1)S(1)}, u32[]{:S(2)}, u32[]{:S(2)}) collective-permute-start(bf16[32,3712]{1,0:T(8,128)(2,1)S(1)} %get-tuple-element.89), channel_id=1, source_target_pairs={{0,56},{4,60},{8,0},{12,4},{16,8},{20,12},{24,16},{28,20},{32,24},... | collective-permute-start | bytes 712712 | tf_op jit(solution)/shard_map/ppermute | solution.py:27
  68.9 10.7 %collective-permute-start.25 = (bf16[32,3712]{1,0:T(8,128)(2,1)S(1)}, bf16[32,3712]{1,0:T(8,128)(2,1)S(1)}, u32[]{:S(2)}, u32[]{:S(2)}) collective-permute-start(bf16[32,3712]{1,0:T(8,128)(2,1)S(1)} %concatenate.107), channel_id=1, source_target_pairs={{0,72},{4,76},{8,80},{12,84},{16,88},{20,92},{24,96},{28,100},{32,... | collective-permute-start | bytes 712712 | tf_op jit(solution)/shard_map/ppermute | solution.py:27

commit v3 on v2

--- a/solution.py
+++ b/solution.py
@@ -17,9 +17,12 @@
     return parts[0] if len(parts) == 1 else jnp.concatenate(parts, axis)
 
 
-def shift(block, dx, dz):
+def shift(block, dx, dz, turn=1):
     pairs = [
-        ((x * NZ + z) * 2 + c, ((x + dx) % NX * NZ + (z + dz) % NZ) * 2 + c)
+        (
+            (x * NZ + z) * 2 + c,
+            ((x + dx * turn**c) % NX * NZ + (z + dz * turn**c) % NZ) * 2 + c,
+        )
         for x in range(NX)
         for z in range(NZ)
         for c in range(2)
@@ -206,10 +209,11 @@
 
     for number, moves in enumerate(ROUNDS):
         sent = [cat([cat([held[src, h] for h in part]) for src, part, _ in load]) for _, load in moves]
+        if number == 4:
+            back = cat([held[(-1, -3), h] for h in F])
+            sent[4] = jnp.where(core == 0, sent[4], back)
         if number == 1:
-            sent, slices, q_slice, query_grads = lax.optimization_barrier(
-                (sent, slices, q_slice, query_grads)
-            )
+            sent, q_slice, query_grads = lax.optimization_barrier((sent, q_slice, query_grads))
             slices, q_mine = [slices, from_col(slices, 2, cols)], columns(query_grads, core)
         if number == 2:
             sent, slices, q_slice, q_mine = lax.optimization_barrier(
@@ -225,7 +229,7 @@
             sent, scores = lax.optimization_barrier((sent, scores))
             work()
         for ((dx, dz), load), block in zip(moves, sent):
-            came = shift(block, dx, dz)
+            came = shift(block, dx, dz, -1 if dx and dz else 1)
             names = [(dst, h) for _, part, dst in load for h in part]
             for i, name in enumerate(names):
                 held[name] = came[i * tokens : (i + 1) * tokens]

time: 114 us -> 114 us (level)
  waiting for transfers between devices: 20 us -> 15.6 us
  blocking collectives: 27.3 us -> 30.7 us
    ppermute x21, waiting for transfers between devices: 18.1 us -> 12.5 us  [shift(): return lax.ppermute(block, 'row', pairs)]
    all_to_all x1, blocking collectives: 27.3 us -> 30.7 us  [body(): arrived = lax.all_to_all(parts, ('row', 'col'), 0, 0, tiled=True)]
    ppermute x3, waiting for transfers between devices: 1.97 us -> 3.15 us  [swap(): return lax.ppermute(block, 'row', [(i, i ^ 1) for i in range(NX * NZ * 2)])]
  transfers between devices with their start and end apart: 26 -> 26, of which waited for: 13 -> 8; matrix products, arithmetic and copies ran while one was open for 4% -> 4% of each run, Pallas kernels for 12% -> 12%
where the time goes in v3:
time: 114 us
  starting transfers between devices  40.2 us (35%)
  blocking collectives  30.7 us (27%)
  Pallas kernels  17.3 us (15%)
  waiting for transfers between devices  15.6 us (14%)
  local copies, waits for them, and re-layouts  6.17 us (5%)
  other arithmetic  2.46 us (2%)
    all_to_all x1, blocking collectives, body(): arrived = lax.all_to_all(parts, ('row', 'col'), 0, 0, tiled=True)  30.7 us
    ppermute x21, starting transfers between devices, shift(): return lax.ppermute(block, 'row', pairs)  27.3 us
    pallas_call x4, Pallas kernels, piece_scores(): pl.pallas_call(functools.partial(scores_kernel, sizes), out_shape=(jax.Sh...  15.2 us
    ppermute x21, waiting for transfers between devices, shift(): return lax.ppermute(block, 'row', pairs)  12.5 us
    ppermute x3, starting transfers between devices, swap(): return lax.ppermute(block, 'row', [(i, i ^ 1) for i in range(NX * NZ * 2)])  8.09 us
    ppermute x2, starting transfers between devices, from_col(): lax.ppermute(block, 'col', [(i, (i - ahead) % cols) for i in range(cols)])  4.84 us
    dynamic_slice x3, local copies, waits for them, and re-layouts, columns(): return lax.dynamic_slice(array, start, array.shape[:-1] + (half,))  3.63 us
    ppermute x3, waiting for transfers between devices, swap(): return lax.ppermute(block, 'row', [(i, i ^ 1) for i in range(NX * NZ * 2)])  3.15 us
  transfers between devices with their start and end apart: 26, of which 8 were waited for; matrix products, arithmetic and copies ran while one was open for 4% of the time, Pallas kernels for 12%

profile of v3, /device:TPU:1, one launch (start us, length us, event | category | flops | bytes accessed | tf_op | source)
XLA Modules:
  0.0 114.0 jit_solution(7368153471504260916)
XLA Ops:
  0.6 0.7 convert_element_type.5
  1.3 1.0 constant_dynamic-slice_fusion.3
  2.4 3.3 %collective-permute-start = (bf16[16,3712]{1,0:T(8,128)(2,1)S(1)}, bf16[16,3712]{1,0:T(8,128)(2,1)S(1)}, u32[]{:S(2)}, u32[]{:S(2)}) collective-permute-start(bf16[16,3712]{1,0:T(8,128)(2,1)S(1)} %pad_maximum_fusion.14), channel_id=1, source_target_pairs={{0,4},{4,0},{8,12},{12,8},{16,20},{20,16},{24,28},{28,24},{32,36},... | collective-permute-start | bytes 356360 | tf_op jit(solution)/shard_map/ppermute | solution.py:34
  5.7 0.1 collective-permute-start.9
  5.9 1.3 %collective-permute-done.9 = bf16[256,128]{1,0:T(8,128)(2,1)S(1)} collective-permute-done((bf16[256,128]{1,0:T(8,128)(2,1)}, bf16[256,128]{1,0:T(8,128)(2,1)S(1)}, u32[]{:S(2)}, u32[]{:S(2)}) %collective-permute-start.9) | collective-permute-done | bytes 65568 | tf_op jit(solution)/shard_map/ppermute | solution.py:34
  7.2 0.9 pad_maximum_fusion.13
  8.1 0.1 collective-permute-start.2
  8.2 2.4 %collective-permute-start.3 = (bf16[32,3712]{1,0:T(8,128)(2,1)S(1)}, bf16[32,3712]{1,0:T(8,128)(2,1)S(1)}, u32[]{:S(2)}, u32[]{:S(2)}) collective-permute-start(bf16[32,3712]{1,0:T(8,128)(2,1)S(1)} %maximum_select_fusion.refs_0_), channel_id=1, source_target_pairs={{0,192},{4,196},{8,200},{12,204},{16,208},{20,212},{24,216},{28,22... | collective-permute-start | bytes 712712 | tf_op jit(solution)/shard_map/ppermute | solution.py:30
  10.5 4.0 %collective-permute-start.4 = (bf16[32,3712]{1,0:T(8,128)(2,1)S(1)}, bf16[32,3712]{1,0:T(8,128)(2,1)S(1)}, u32[]{:S(2)}, u32[]{:S(2)}) collective-permute-start(bf16[32,3712]{1,0:T(8,128)(2,1)S(1)} %maximum_select_fusion.refs_0_), channel_id=1, source_target_pairs={{0,56},{4,60},{8,0},{12,4},{16,8},{20,12},{24,16},{28,20},{32,24},... | collective-permute-start | bytes 712712 | tf_op jit(solution)/shard_map/ppermute | solution.py:30
  14.6 2.7 %collective-permute-start.10 = (bf16[256,256]{1,0:T(8,128)(2,1)S(1)}, bf16[256,256]{1,0:T(8,128)(2,1)S(1)}, u32[]{:S(2)}, u32[]{:S(2)}) collective-permute-start(bf16[256,256]{1,0:T(8,128)(2,1)S(1)} %pad_maximum_fusion.13), channel_id=1, source_target_pairs={{0,3},{1,0},{2,1},{3,2},{4,7},{5,4},{6,5},{7,6},{8,11},{9,8},{10,9... | collective-permute-start | bytes 393224 | tf_op jit(solution)/shard_map/ppermute | solution.py:38
  17.3 2.4 %constant_dynamic-slice_fusion.1 = bf16[4,128,3584]{2,1,0:T(8,128)(2,1)S(1)} fusion(bf16[4,128,7168]{2,1,0:T(8,128)(2,1)} %param.7, s32[]{:T(128)S(6)} %select_n.22), kind=kLoop, calls=%fused_computation.33 | loop fusion | bytes 7340036 | tf_op jit(solution)/shard_map/dynamic_slice | solution.py:178
  19.8 2.1 %collective-permute-start.11 = (bf16[512,256]{1,0:T(8,128)(2,1)S(1)}, bf16[512,256]{1,0:T(8,128)(2,1)S(1)}, u32[]{:S(2)}, u32[]{:S(2)}) collective-permute-start(bf16[512,256]{1,0:T(8,128)(2,1)S(1)} %constant_dynamic-update-slice_fusion.mine), channel_id=1, source_target_pairs={{0,2},{1,3},{2,0},{3,1},{4,6},{5,7},{6,4},{7,5},{8,10},{9,11},{10,... | collective-permute-start | bytes 786440 | tf_op jit(solution)/shard_map/ppermute | solution.py:38
  22.1 1.3 %collective-permute-start.6 = (bf16[64,3712]{1,0:T(8,128)(2,1)S(1)}, bf16[64,3712]{1,0:T(8,128)(2,1)S(1)}, u32[]{:S(2)}, u32[]{:S(2)}) collective-permute-start(bf16[64,3712]{1,0:T(8,128)(2,1)S(1)} %pad_maximum_fusion.1), channel_id=1, source_target_pairs={{0,56},{4,60},{8,0},{12,4},{16,8},{20,12},{24,16},{28,20},{32,24},... | collective-permute-start | bytes 1425416 | tf_op jit(solution)/shard_map/ppermute | solution.py:30
  23.4 0.3 collective-permute-start.7
  23.7 2.4 %collective-permute-start.8 = (bf16[48,3712]{1,0:T(8,128)(2,1)S(1)}, bf16[48,3712]{1,0:T(8,128)(2,1)S(1)}, u32[]{:S(2)}, u32[]{:S(2)}) collective-permute-start(bf16[48,3712]{1,0:T(8,128)(2,1)S(1)} %pad_maximum_fusion.7), channel_id=1, source_target_pairs={{0,192},{4,196},{8,200},{12,204},{16,208},{20,212},{24,216},{28,22... | collective-permute-start | bytes 1069064 | tf_op jit(solution)/shard_map/ppermute | solution.py:30
  26.1 0.2 constant_dynamic-slice_fusion.q_mine
  26.3 4.7 %collective-permute-done.8.refs_6_ = bf16[48,3712]{1,0:T(8,128)(2,1)S(1)} collective-permute-done((bf16[48,3712]{1,0:T(8,128)(2,1)S(1)}, bf16[48,3712]{1,0:T(8,128)(2,1)S(1)}, u32[]{:S(2)}, u32[]{:S(2)}) %collective-permute-start.8) | collective-permute-done | bytes 356384 | tf_op jit(solution)/shard_map/ppermute | solution.py:30
  31.0 3.0 %collective-permute-done.5.refs_5_ = bf16[48,3712]{1,0:T(8,128)(2,1)S(1)} collective-permute-done((bf16[48,3712]{1,0:T(8,128)(2,1)S(1)}, bf16[48,3712]{1,0:T(8,128)(2,1)S(1)}, u32[]{:S(2)}, u32[]{:S(2)}) %collective-permute-start.5) | collective-permute-done | bytes 356384 | tf_op jit(solution)/shard_map/ppermute | solution.py:30
  34.1 0.5 collective-permute-done.7.refs_0_
  34.7 2.1 %collective-permute-start.13 = (bf16[64,3712]{1,0:T(8,128)(2,1)S(1)}, bf16[64,3712]{1,0:T(8,128)(2,1)S(1)}, u32[]{:S(2)}, u32[]{:S(2)}) collective-permute-start(bf16[64,3712]{1,0:T(8,128)(2,1)S(1)} %collective-permute-done.6.refs_1_), channel_id=1, source_target_pairs={{0,56},{4,60},{8,0},{12,4},{16,8},{20,12},{24,16},{28,20},{32,24},... | collective-permute-start | bytes 1425416 | tf_op jit(solution)/shard_map/ppermute | solution.py:30
  36.8 0.7 collective-permute-start.15
  37.5 0.8 collective-permute-start.12
  38.3 0.4 collective-permute-start.14
  38.6 4.7 %collective-permute-start.16 = (bf16[4,128,3584]{2,1,0:T(8,128)(2,1)S(1)}, bf16[4,128,3584]{2,1,0:T(8,128)(2,1)S(1)}, u32[]{:S(2)}, u32[]{:S(2)}) collective-permute-start(bf16[4,128,3584]{2,1,0:T(8,128)(2,1)S(1)} %constant_dynamic-slice_fusion.1), channel_id=1, source_target_pairs={{0,4},{4,0},{8,12},{12,8},{16,20},{20,16},{24,28},{28,24},{32,36},... | collective-permute-start | bytes 11010056 | tf_op jit(solution)/shard_map/ppermute | solution.py:34
  43.3 2.2 %weights.1 = (f32[256,256]{1,0:T(8,128)S(1)}, f32[256,256]{1,0:T(8,128)S(1)}, f32[256,256]{1,0:T(8,128)S(1)}, f32[256,256]{1,0:T(8,128)S(1)}) custom-call(s32[2]{0:T(128)S(1)} %pad_add_fusion.where, bf16[512,256]{1,0:T(8,128)(2,1)S(1)} %constant_dynamic-update-slice_fusion.mine, bf16[512,256]{1,0:T(8,128)(2,1)S(1)} %collective-permute-done.11.ahead), custom_call_target="tpu_custom_call" | custom-call | tf_op jit(solution)/shard_map/weights/pallas_call | solution.py:94
  45.6 1.4 %collective-permute-done.12.refs_2_ = bf16[64,3712]{1,0:T(8,128)(2,1)S(1)} collective-permute-done((bf16[64,3712]{1,0:T(8,128)(2,1)S(1)}, bf16[64,3712]{1,0:T(8,128)(2,1)S(1)}, u32[]{:S(2)}, u32[]{:S(2)}) %collective-permute-start.12) | collective-permute-done | bytes 475168 | tf_op jit(solution)/shard_map/ppermute | solution.py:30
  47.0 0.3 collective-permute-done.14.refs_0_
  47.5 1.9 %collective-permute-done.16.q_other = bf16[4,128,3584]{2,1,0:T(8,128)(2,1)S(1)} collective-permute-done((bf16[4,128,3584]{2,1,0:T(8,128)(2,1)S(1)}, bf16[4,128,3584]{2,1,0:T(8,128)(2,1)S(1)}, u32[]{:S(2)}, u32[]{:S(2)}) %collective-permute-start.16) | collective-permute-done | bytes 3670048 | tf_op jit(solution)/shard_map/ppermute | solution.py:34
  49.3 2.8 %collective-permute-start.20 = (bf16[64,3712]{1,0:T(8,128)(2,1)S(1)}, bf16[64,3712]{1,0:T(8,128)(2,1)S(1)}, u32[]{:S(2)}, u32[]{:S(2)}) collective-permute-start(bf16[64,3712]{1,0:T(8,128)(2,1)S(1)} %pad_maximum_fusion.5), channel_id=1, source_target_pairs={{0,192},{4,196},{8,200},{12,204},{16,208},{20,212},{24,216},{28,22... | collective-permute-start | bytes 1425416 | tf_op jit(solution)/shard_map/ppermute | solution.py:30
  52.1 2.9 %collective-permute-start.18 = (bf16[48,3712]{1,0:T(8,128)(2,1)S(1)}, bf16[48,3712]{1,0:T(8,128)(2,1)S(1)}, u32[]{:S(2)}, u32[]{:S(2)}) collective-permute-start(bf16[48,3712]{1,0:T(8,128)(2,1)S(1)} %slice.172), channel_id=1, source_target_pairs={{0,56},{4,60},{8,0},{12,4},{16,8},{20,12},{24,16},{28,20},{32,24},... | collective-permute-start | bytes 1069064 | tf_op jit(solution)/shard_map/ppermute | solution.py:30
  55.0 3.5 %scores.5 = (f32[8,256]{1,0:T(8,128)S(1)}, f32[8,128]{1,0:T(8,128)S(1)}) custom-call(bf16[4,128,3584]{2,1,0:T(8,128)(2,1)S(1)} %constant_dynamic-slice_fusion.q_mine, bf16[4,128,3584]{2,1,0:T(8,128)(2,1)S(1)} %collective-permute-done.16.q_other, f32[256,256]{1,0:T(8,128)S(1)} %get-tuple-element.77.weights, ...), custom_call_target="tpu_custom_call" | custom-call | flops 1879048192 | bytes 9175040 | tf_op jit(solution)/shard_map/scores/pallas_call | solution.py:144
  58.4 4.1 %scores.4 = (f32[8,256]{1,0:T(8,128)S(1)}, f32[8,128]{1,0:T(8,128)S(1)}) custom-call(bf16[4,128,3584]{2,1,0:T(8,128)(2,1)S(1)} %constant_dynamic-slice_fusion.q_mine, bf16[4,128,3584]{2,1,0:T(8,128)(2,1)S(1)} %collective-permute-done.16.q_other, f32[256,256]{1,0:T(8,128)S(1)} %get-tuple-element.75.weights, bf16[32,3712]{1,0:T(8,128)(2,1)S(1)} %maximum_select_fusion.refs_0_, ...), custom_call_target="tpu_custom_call" | custom-call | flops 1879048192 | bytes 9175040 | tf_op jit(solution)/shard_map/scores/pallas_call | solution.py:144
  62.9 0.1 collective-permute-start.21
  63.0 2.7 %collective-permute-start.22 = (bf16[32,3712]{1,0:T(8,128)(2,1)S(1)}, bf16[32,3712]{1,0:T(8,128)(2,1)S(1)}, u32[]{:S(2)}, u32[]{:S(2)}) collective-permute-start(bf16[32,3712]{1,0:T(8,128)(2,1)S(1)} %get-tuple-element.85), channel_id=1, source_target_pairs={{0,192},{4,196},{8,200},{12,204},{16,208},{20,212},{24,216},{28,22... | collective-permute-start | bytes 712712 | tf_op jit(solution)/shard_map/ppermute | solution.py:30
  65.6 2.7 %collective-permute-start.24 = (bf16[32,3712]{1,0:T(8,128)(2,1)S(1)}, bf16[32,3712]{1,0:T(8,128)(2,1)S(1)}, u32[]{:S(2)}, u32[]{:S(2)}) collective-permute-start(bf16[32,3712]{1,0:T(8,128)(2,1)S(1)} %get-tuple-element.87), channel_id=1, source_target_pairs={{0,56},{4,60},{8,0},{12,4},{16,8},{20,12},{24,16},{28,20},{32,24},... | collective-permute-start | bytes 712712 | tf_op jit(solution)/shard_map/ppermute | solution.py:30
  68.3 1.9 %collective-permute-start.25 = (bf16[32,3712]{1,0:T(8,128)(2,1)S(1)}, bf16[32,3712]{1,0:T(8,128)(2,1)S(1)}, u32[]{:S(2)}, u32[]{:S(2)}) collective-permute-start(bf16[32,3712]{1,0:T(8,128)(2,1)S(1)} %slice_select_fusion), channel_id=1, source_target_pairs={{0,72},{4,252},{8,80},{12,196},{16,88},{20,204},{24,96},{28,212},{... | collective-permute-start | bytes 712712 | tf_op jit(solution)/shard_map/ppermute | solution.py:30
  70.2 3.5 %scores.6 = (f32[8,256]{1,0:T(8,128)S(1)}, f32[8,128]{1,0:T(8,128)S(1)}) custom-call(bf16[4,128,3584]{2,1,0:T(8,128)(2,1)S(1)} %constant_dynamic-slice_fusion.q_mine, bf16[4,128,3584]{2,1,0:T(8,128)(2,1)S(1)} %collective-permute-done.16.q_other, f32[256,256]{1,0:T(8,128)S(1)} %get-tuple-element.81.weights, ...), custom_call_target="tpu_custom_call" | custom-call | flops 1879048192 | bytes 9175040 | tf_op jit(solution)/shard_map/scores/pallas_call | solution.py:144
  73.7 2.6 %collective-permute-done.25.refs_6_ = bf16[32,3712]{1,0:T(8,128)(2,1)S(1)} collective-permute-done((bf16[32,3712]{1,0:T(8,128)(2,1)S(1)}, bf16[32,3712]{1,0:T(8,128)(2,1)S(1)}, u32[]{:S(2)}, u32[]{:S(2)}) %collective-permute-start.25) | collective-permute-done | bytes 237600 | tf_op jit(solution)/shard_map/ppermute | solution.py:30
  76.3 4.1 %scores.7 = (f32[8,256]{1,0:T(8,128)S(1)}, f32[8,128]{1,0:T(8,128)S(1)}) custom-call(bf16[4,128,3584]{2,1,0:T(8,128)(2,1)S(1)} %constant_dynamic-slice_fusion.q_mine, bf16[4,128,3584]{2,1,0:T(8,128)(2,1)S(1)} %collective-permute-done.16.q_other, f32[256,256]{1,0:T(8,128)S(1)} %get-tuple-element.83.weights, ...), custom_call_target="tpu_custom_call" | custom-call | flops 1879048192 | bytes 9175040 | tf_op jit(solution)/shard_map/scores/pallas_call | solution.py:144
  80.5 0.1 reshape.43
  80.6 0.1 reshape.40
  80.7 0.1 copy.10
  80.8 0.3 fusion.1
  81.2 0.4 all_to_all.8
  81.6 30.7 %all_to_all.10 = f32[256,1,192]{2,1,0:T(1,128)S(1)} all-to-all(f32[256,1,192]{2,1,0:T(1,128)S(1)} %all_to_all.8), channel_id=1, replica_groups=mesh['row'=64,'col'=4] {'row','col'}, dimensions={0} | all-to-all | bytes 393216 | tf_op jit(solution)/shard_map/all_to_all | solution.py:256
  112.3 0.3 reduce_sum.9
  112.6 0.7 reshape.41
  113.3 0.7 reshape.42
  (77 shorter events, 1.3 us)
Async XLA Ops:
  2.4 5.7 %collective-permute-start = (bf16[16,3712]{1,0:T(8,128)(2,1)S(1)}, bf16[16,3712]{1,0:T(8,128)(2,1)S(1)}, u32[]{:S(2)}, u32[]{:S(2)}) collective-permute-start(bf16[16,3712]{1,0:T(8,128)(2,1)S(1)} %pad_maximum_fusion.14), channel_id=1, source_target_pairs={{0,4},{4,0},{8,12},{12,8},{16,20},{20,16},{24,28},{28,24},{32,36},... | collective-permute-start | bytes 356360 | tf_op jit(solution)/shard_map/ppermute | solution.py:34
  5.7 1.5 %collective-permute-start.9 = (bf16[256,128]{1,0:T(8,128)(2,1)}, bf16[256,128]{1,0:T(8,128)(2,1)S(1)}, u32[]{:S(2)}, u32[]{:S(2)}) collective-permute-start(bf16[256,128]{1,0:T(8,128)(2,1)} %param.8), channel_id=1, source_target_pairs={{0,4},{4,0},{8,12},{12,8},{16,20},{20,16},{24,28},{28,24},{32,36},... | collective-permute-start | bytes 196616 | tf_op jit(solution)/shard_map/ppermute | solution.py:34
  8.1 13.9 %collective-permute-start.2 = (bf16[32,3712]{1,0:T(8,128)(2,1)S(1)}, bf16[32,3712]{1,0:T(8,128)(2,1)S(1)}, u32[]{:S(2)}, u32[]{:S(2)}) collective-permute-start(bf16[32,3712]{1,0:T(8,128)(2,1)S(1)} %maximum_select_fusion.refs_0_), channel_id=1, source_target_pairs={{0,8},{4,12},{8,16},{12,20},{16,24},{20,28},{24,32},{28,36},{32,40... | collective-permute-start | bytes 712712 | tf_op jit(solution)/shard_map/ppermute | solution.py:30
  8.2 13.7 %collective-permute-start.3 = (bf16[32,3712]{1,0:T(8,128)(2,1)S(1)}, bf16[32,3712]{1,0:T(8,128)(2,1)S(1)}, u32[]{:S(2)}, u32[]{:S(2)}) collective-permute-start(bf16[32,3712]{1,0:T(8,128)(2,1)S(1)} %maximum_select_fusion.refs_0_), channel_id=1, source_target_pairs={{0,192},{4,196},{8,200},{12,204},{16,208},{20,212},{24,216},{28,22... | collective-permute-start | bytes 712712 | tf_op jit(solution)/shard_map/ppermute | solution.py:30
  10.5 11.4 %collective-permute-start.1 = (bf16[32,3712]{1,0:T(8,128)(2,1)S(1)}, bf16[32,3712]{1,0:T(8,128)(2,1)S(1)}, u32[]{:S(2)}, u32[]{:S(2)}) collective-permute-start(bf16[32,3712]{1,0:T(8,128)(2,1)S(1)} %maximum_select_fusion.refs_0_), channel_id=1, source_target_pairs={{0,64},{4,68},{8,72},{12,76},{16,80},{20,84},{24,88},{28,92},{32,9... | collective-permute-start | bytes 712712 | tf_op jit(solution)/shard_map/ppermute | solution.py:30
  10.5 11.5 %collective-permute-start.4 = (bf16[32,3712]{1,0:T(8,128)(2,1)S(1)}, bf16[32,3712]{1,0:T(8,128)(2,1)S(1)}, u32[]{:S(2)}, u32[]{:S(2)}) collective-permute-start(bf16[32,3712]{1,0:T(8,128)(2,1)S(1)} %maximum_select_fusion.refs_0_), channel_id=1, source_target_pairs={{0,56},{4,60},{8,0},{12,4},{16,8},{20,12},{24,16},{28,20},{32,24},... | collective-permute-start | bytes 712712 | tf_op jit(solution)/shard_map/ppermute | solution.py:30
  14.6 5.2 %collective-permute-start.10 = (bf16[256,256]{1,0:T(8,128)(2,1)S(1)}, bf16[256,256]{1,0:T(8,128)(2,1)S(1)}, u32[]{:S(2)}, u32[]{:S(2)}) collective-permute-start(bf16[256,256]{1,0:T(8,128)(2,1)S(1)} %pad_maximum_fusion.13), channel_id=1, source_target_pairs={{0,3},{1,0},{2,1},{3,2},{4,7},{5,4},{6,5},{7,6},{8,11},{9,8},{10,9... | collective-permute-start | bytes 393224 | tf_op jit(solution)/shard_map/ppermute | solution.py:38
  17.3 8.8 %copy-start = (bf16[4,128,7168]{2,1,0:T(8,128)(2,1)S(1)}, bf16[4,128,7168]{2,1,0:T(8,128)(2,1)}, u32[]{:S(2)}) copy-start(bf16[4,128,7168]{2,1,0:T(8,128)(2,1)} %param.7) | copy-start | bytes 22020100
  19.8 14.9 %collective-permute-start.11 = (bf16[512,256]{1,0:T(8,128)(2,1)S(1)}, bf16[512,256]{1,0:T(8,128)(2,1)S(1)}, u32[]{:S(2)}, u32[]{:S(2)}) collective-permute-start(bf16[512,256]{1,0:T(8,128)(2,1)S(1)} %constant_dynamic-update-slice_fusion.mine), channel_id=1, source_target_pairs={{0,2},{1,3},{2,0},{3,1},{4,6},{5,7},{6,4},{7,5},{8,10},{9,11},{10,... | collective-permute-start | bytes 786440 | tf_op jit(solution)/shard_map/ppermute | solution.py:38
  22.1 11.9 %collective-permute-start.6 = (bf16[64,3712]{1,0:T(8,128)(2,1)S(1)}, bf16[64,3712]{1,0:T(8,128)(2,1)S(1)}, u32[]{:S(2)}, u32[]{:S(2)}) collective-permute-start(bf16[64,3712]{1,0:T(8,128)(2,1)S(1)} %pad_maximum_fusion.1), channel_id=1, source_target_pairs={{0,56},{4,60},{8,0},{12,4},{16,8},{20,12},{24,16},{28,20},{32,24},... | collective-permute-start | bytes 1425416 | tf_op jit(solution)/shard_map/ppermute | solution.py:30
  23.4 11.2 %collective-permute-start.7 = (bf16[64,3712]{1,0:T(8,128)(2,1)S(1)}, bf16[64,3712]{1,0:T(8,128)(2,1)S(1)}, u32[]{:S(2)}, u32[]{:S(2)}) collective-permute-start(bf16[64,3712]{1,0:T(8,128)(2,1)S(1)} %pad_maximum_fusion), channel_id=1, source_target_pairs={{0,8},{4,12},{8,16},{12,20},{16,24},{20,28},{24,32},{28,36},{32,40... | collective-permute-start | bytes 1425416 | tf_op jit(solution)/shard_map/ppermute | solution.py:30
  23.7 7.4 %collective-permute-start.8 = (bf16[48,3712]{1,0:T(8,128)(2,1)S(1)}, bf16[48,3712]{1,0:T(8,128)(2,1)S(1)}, u32[]{:S(2)}, u32[]{:S(2)}) collective-permute-start(bf16[48,3712]{1,0:T(8,128)(2,1)S(1)} %pad_maximum_fusion.7), channel_id=1, source_target_pairs={{0,192},{4,196},{8,200},{12,204},{16,208},{20,212},{24,216},{28,22... | collective-permute-start | bytes 1069064 | tf_op jit(solution)/shard_map/ppermute | solution.py:30
  26.1 8.0 %collective-permute-start.5 = (bf16[48,3712]{1,0:T(8,128)(2,1)S(1)}, bf16[48,3712]{1,0:T(8,128)(2,1)S(1)}, u32[]{:S(2)}, u32[]{:S(2)}) collective-permute-start(bf16[48,3712]{1,0:T(8,128)(2,1)S(1)} %pad_maximum_fusion.6), channel_id=1, source_target_pairs={{0,64},{4,68},{8,72},{12,76},{16,80},{20,84},{24,88},{28,92},{32,9... | collective-permute-start | bytes 1069064 | tf_op jit(solution)/shard_map/ppermute | solution.py:30
  34.7 10.8 %collective-permute-start.13 = (bf16[64,3712]{1,0:T(8,128)(2,1)S(1)}, bf16[64,3712]{1,0:T(8,128)(2,1)S(1)}, u32[]{:S(2)}, u32[]{:S(2)}) collective-permute-start(bf16[64,3712]{1,0:T(8,128)(2,1)S(1)} %collective-permute-done.6.refs_1_), channel_id=1, source_target_pairs={{0,56},{4,60},{8,0},{12,4},{16,8},{20,12},{24,16},{28,20},{32,24},... | collective-permute-start | bytes 1425416 | tf_op jit(solution)/shard_map/ppermute | solution.py:30
  36.8 8.8 %collective-permute-start.15 = (bf16[64,3712]{1,0:T(8,128)(2,1)S(1)}, bf16[64,3712]{1,0:T(8,128)(2,1)S(1)}, u32[]{:S(2)}, u32[]{:S(2)}) collective-permute-start(bf16[64,3712]{1,0:T(8,128)(2,1)S(1)} %pad_maximum_fusion.3), channel_id=1, source_target_pairs={{0,192},{4,196},{8,200},{12,204},{16,208},{20,212},{24,216},{28,22... | collective-permute-start | bytes 1425416 | tf_op jit(solution)/shard_map/ppermute | solution.py:30
  37.5 9.5 %collective-permute-start.12 = (bf16[64,3712]{1,0:T(8,128)(2,1)S(1)}, bf16[64,3712]{1,0:T(8,128)(2,1)S(1)}, u32[]{:S(2)}, u32[]{:S(2)}) collective-permute-start(bf16[64,3712]{1,0:T(8,128)(2,1)S(1)} %pad_maximum_fusion.2), channel_id=1, source_target_pairs={{0,64},{4,68},{8,72},{12,76},{16,80},{20,84},{24,88},{28,92},{32,9... | collective-permute-start | bytes 1425416 | tf_op jit(solution)/shard_map/ppermute | solution.py:30
  38.3 9.0 %collective-permute-start.14 = (bf16[64,3712]{1,0:T(8,128)(2,1)S(1)}, bf16[64,3712]{1,0:T(8,128)(2,1)S(1)}, u32[]{:S(2)}, u32[]{:S(2)}) collective-permute-start(bf16[64,3712]{1,0:T(8,128)(2,1)S(1)} %collective-permute-done.7.refs_0_), channel_id=1, source_target_pairs={{0,8},{4,12},{8,16},{12,20},{16,24},{20,28},{24,32},{28,36},{32,40... | collective-permute-start | bytes 1425416 | tf_op jit(solution)/shard_map/ppermute | solution.py:30
  38.6 10.7 %collective-permute-start.16 = (bf16[4,128,3584]{2,1,0:T(8,128)(2,1)S(1)}, bf16[4,128,3584]{2,1,0:T(8,128)(2,1)S(1)}, u32[]{:S(2)}, u32[]{:S(2)}) collective-permute-start(bf16[4,128,3584]{2,1,0:T(8,128)(2,1)S(1)} %constant_dynamic-slice_fusion.1), channel_id=1, source_target_pairs={{0,4},{4,0},{8,12},{12,8},{16,20},{20,16},{24,28},{28,24},{32,36},... | collective-permute-start | bytes 11010056 | tf_op jit(solution)/shard_map/ppermute | solution.py:34
  49.3 13.3 %collective-permute-start.19 = (bf16[48,3712]{1,0:T(8,128)(2,1)S(1)}, bf16[48,3712]{1,0:T(8,128)(2,1)S(1)}, u32[]{:S(2)}, u32[]{:S(2)}) collective-permute-start(bf16[48,3712]{1,0:T(8,128)(2,1)S(1)} %pad_maximum_fusion.8), channel_id=1, source_target_pairs={{0,8},{4,12},{8,16},{12,20},{16,24},{20,28},{24,32},{28,36},{32,40... | collective-permute-start | bytes 1069064 | tf_op jit(solution)/shard_map/ppermute | solution.py:30
  49.3 13.4 %collective-permute-start.17 = (bf16[64,3712]{1,0:T(8,128)(2,1)S(1)}, bf16[64,3712]{1,0:T(8,128)(2,1)S(1)}, u32[]{:S(2)}, u32[]{:S(2)}) collective-permute-start(bf16[64,3712]{1,0:T(8,128)(2,1)S(1)} %pad_maximum_fusion.4), channel_id=1, source_target_pairs={{0,64},{4,68},{8,72},{12,76},{16,80},{20,84},{24,88},{28,92},{32,9... | collective-permute-start | bytes 1425416 | tf_op jit(solution)/shard_map/ppermute | solution.py:30
  49.3 13.3 %collective-permute-start.20 = (bf16[64,3712]{1,0:T(8,128)(2,1)S(1)}, bf16[64,3712]{1,0:T(8,128)(2,1)S(1)}, u32[]{:S(2)}, u32[]{:S(2)}) collective-permute-start(bf16[64,3712]{1,0:T(8,128)(2,1)S(1)} %pad_maximum_fusion.5), channel_id=1, source_target_pairs={{0,192},{4,196},{8,200},{12,204},{16,208},{20,212},{24,216},{28,22... | collective-permute-start | bytes 1425416 | tf_op jit(solution)/shard_map/ppermute | solution.py:30
  52.1 10.6 %collective-permute-start.18 = (bf16[48,3712]{1,0:T(8,128)(2,1)S(1)}, bf16[48,3712]{1,0:T(8,128)(2,1)S(1)}, u32[]{:S(2)}, u32[]{:S(2)}) collective-permute-start(bf16[48,3712]{1,0:T(8,128)(2,1)S(1)} %slice.172), channel_id=1, source_target_pairs={{0,56},{4,60},{8,0},{12,4},{16,8},{20,12},{24,16},{28,20},{32,24},... | collective-permute-start | bytes 1069064 | tf_op jit(solution)/shard_map/ppermute | solution.py:30
  62.6 7.6 %copy-start.1 = (s32[64]{0:T(128)S(1)}, s32[64]{0:T(128)}, u32[]{:S(2)}) copy-start(s32[64]{0:T(128)} %constant.51.clone) | copy-start | bytes 772
  62.6 7.6 %copy-start.2 = (s32[64]{0:T(128)S(1)}, s32[64]{0:T(128)}, u32[]{:S(2)}) copy-start(s32[64]{0:T(128)} %constant.52.clone) | copy-start | bytes 772
  62.6 7.6 %copy-start.3 = (s32[64]{0:T(128)S(1)}, s32[64]{0:T(128)}, u32[]{:S(2)}) copy-start(s32[64]{0:T(128)} %constant.53.clone) | copy-start | bytes 772
  62.9 10.8 %collective-permute-start.21 = (bf16[32,3712]{1,0:T(8,128)(2,1)S(1)}, bf16[32,3712]{1,0:T(8,128)(2,1)S(1)}, u32[]{:S(2)}, u32[]{:S(2)}) collective-permute-start(bf16[32,3712]{1,0:T(8,128)(2,1)S(1)} %get-tuple-element.84), channel_id=1, source_target_pairs={{0,64},{4,68},{8,72},{12,76},{16,80},{20,84},{24,88},{28,92},{32,9... | collective-permute-start | bytes 712712 | tf_op jit(solution)/shard_map/ppermute | solution.py:30
  63.0 10.7 %collective-permute-start.22 = (bf16[32,3712]{1,0:T(8,128)(2,1)S(1)}, bf16[32,3712]{1,0:T(8,128)(2,1)S(1)}, u32[]{:S(2)}, u32[]{:S(2)}) collective-permute-start(bf16[32,3712]{1,0:T(8,128)(2,1)S(1)} %get-tuple-element.85), channel_id=1, source_target_pairs={{0,192},{4,196},{8,200},{12,204},{16,208},{20,212},{24,216},{28,22... | collective-permute-start | bytes 712712 | tf_op jit(solution)/shard_map/ppermute | solution.py:30
  65.6 8.1 %collective-permute-start.23 = (bf16[32,3712]{1,0:T(8,128)(2,1)S(1)}, bf16[32,3712]{1,0:T(8,128)(2,1)S(1)}, u32[]{:S(2)}, u32[]{:S(2)}) collective-permute-start(bf16[32,3712]{1,0:T(8,128)(2,1)S(1)} %get-tuple-element.86), channel_id=1, source_target_pairs={{0,8},{4,12},{8,16},{12,20},{16,24},{20,28},{24,32},{28,36},{32,40... | collective-permute-start | bytes 712712 | tf_op jit(solution)/shard_map/ppermute | solution.py:30
  65.6 8.1 %collective-permute-start.24 = (bf16[32,3712]{1,0:T(8,128)(2,1)S(1)}, bf16[32,3712]{1,0:T(8,128)(2,1)S(1)}, u32[]{:S(2)}, u32[]{:S(2)}) collective-permute-start(bf16[32,3712]{1,0:T(8,128)(2,1)S(1)} %get-tuple-element.87), channel_id=1, source_target_pairs={{0,56},{4,60},{8,0},{12,4},{16,8},{20,12},{24,16},{28,20},{32,24},... | collective-permute-start | bytes 712712 | tf_op jit(solution)/shard_map/ppermute | solution.py:30
  68.3 8.0 %collective-permute-start.25 = (bf16[32,3712]{1,0:T(8,128)(2,1)S(1)}, bf16[32,3712]{1,0:T(8,128)(2,1)S(1)}, u32[]{:S(2)}, u32[]{:S(2)}) collective-permute-start(bf16[32,3712]{1,0:T(8,128)(2,1)S(1)} %slice_select_fusion), channel_id=1, source_target_pairs={{0,72},{4,252},{8,80},{12,196},{16,88},{20,204},{24,96},{28,212},{... | collective-permute-start | bytes 712712 | tf_op jit(solution)/shard_map/ppermute | solution.py:30
